TPU v7x, 32 devices: a whole 2x2x4 slice. The times are simulated.
32 devices in a mesh: parts: 2 (over y), replica: 4 (over z), tensor: 4 (over x, core).
Axes of the slice: x: 2, y: 2, z: 4, core: 2. Of those that a mesh axis runs over, the one named last changes fastest.
Arguments:
- tokens: bfloat16 [4096, 8192], P(('parts', 'replica'), 'tensor'), parts along dimension 0, may hold values from -6 to 6
- value_weight: bfloat16 [8192, 512], P('tensor'), may hold values from -0.0625 to 0.0625
- down_factor: bfloat16 [256, 8192, 64], P(('parts', 'replica'), 'tensor'), parts along dimension 0, may hold values from -0.0625 to 0.0625
- up_factor: bfloat16 [256, 64, 512], P(('parts', 'replica'), None, 'tensor'), parts along dimension 0, may hold values from -0.75 to 0.75
- request_adapter: int32 [4096], P('parts'), parts along dimension 0, may hold values from 0 to 127, as said below
- adapter_slot_map: int32 [256], P('parts'), parts along dimension 0, may hold values from 0 to 127, as said below
Outputs:
- values_out: bfloat16 [4096, 512], P(('parts', 'replica'), 'tensor'), parts along dimension 0
There are 2 independent parts, one for each index of `parts`. A program takes and returns all parts, laid end to end along the dimension named above; an argument that names none is the same for every part. Nothing has to cross between parts.
Inputs may be any that keep to these rules, and one draw needn't show every extreme that they name: `request_adapter`: replica r holds requests r * 512 to (r + 1) * 512 - 1, and pool slots r * 32 to (r + 1) * 32 - 1. Of the requests of one replica, at most 256 have adapters whose slots lie on one replica; in every draw some replicas receive exactly 256 from every replica. `adapter_slot_map`: A permutation.
All inputs are finite; a program needn't handle non-finite values.
Results may differ from a plain program's by a relative error of at most 0.0043.
Values may be sent and summed in bfloat16 or wider, within the bound.
No kernel may reach another device: no remote copies, remote signals or barrier semaphores. Data moves between devices by JAX's collectives and lax.ppermute only.
A program may use at most 128 MiB of HBM per device.

v0:
```python
import functools

import jax
import jax.numpy as jnp
from jax import lax
from jax.experimental import pallas as pl
from jax.experimental.pallas import tpu as pltpu
from jax.sharding import PartitionSpec as P

ADAPTER_SCALE = 0.5
MAX_OWNERS = 8
COPIES = 8
GROUPS = 4
BLOCK = 4
BRIEF = pl.CostEstimate(flops=0, bytes_accessed=0, transcendentals=0)
VMEM_BYTES = 40 * 1024 * 1024
NT = (((1,), (1,)), ((), ()))
TN = (((0,), (0,)), ((), ()))


def plain_body(tokens, value_weight, down_factor, up_factor, request_adapter, adapter_slot_map):
    row_count, quarter = tokens.shape
    owners = lax.axis_size("replica")
    local_adapters = down_factor.shape[0]
    output_piece = up_factor.shape[2]
    capacity = 2 * row_count // owners
    my_index = lax.axis_index("replica")
    pool_slot = jnp.take(adapter_slot_map, request_adapter)
    owner_grid = (pool_slot // local_adapters).reshape(owners, row_count)
    local_grid = (pool_slot % local_adapters).reshape(owners, row_count)
    my_owner = lax.dynamic_slice_in_dim(owner_grid, my_index, 1, 0)[0]
    owner_hot = (my_owner[:, None] == jnp.arange(owners)[None, :]).astype(jnp.int32)
    my_rank = jnp.sum(jnp.cumsum(owner_hot, axis=0) * owner_hot, axis=1) - 1
    position = my_owner * capacity + my_rank
    packer = (jnp.arange(owners * capacity)[:, None] == position[None, :]).astype(jnp.bfloat16)
    outgoing = jnp.dot(packer, tokens, preferred_element_type=jnp.float32).astype(jnp.bfloat16)
    outgoing = outgoing.reshape(owners, capacity, quarter)
    partial_base = jnp.dot(tokens, value_weight, preferred_element_type=jnp.float32)
    arrived = lax.all_to_all(outgoing, "replica", split_axis=0, concat_axis=0, tiled=True)
    mine = (owner_grid == my_index).astype(jnp.int32)
    recv_rank = jnp.cumsum(mine, axis=1) - 1
    selector = (
        (recv_rank[:, None, :] == jnp.arange(capacity)[None, :, None]) & (mine[:, None, :] > 0)
    ).astype(jnp.int32)
    slot_local = jnp.sum(selector * local_grid[:, None, :], axis=2).reshape(owners * capacity)
    sort_order = jnp.argsort(slot_local, stable=True)
    inverse_order = jnp.argsort(sort_order)
    group_row_count = jnp.sum(
        (slot_local[:, None] == jnp.arange(local_adapters)[None, :]).astype(jnp.int32), axis=0
    )
    rows_by_adapter = jnp.take(arrived.reshape(owners * capacity, quarter), sort_order, axis=0)
    partial_rank = lax.ragged_dot(
        rows_by_adapter, down_factor, group_row_count, preferred_element_type=jnp.float32
    )
    rank_projected = lax.psum(partial_rank, "tensor").astype(jnp.bfloat16)
    sorted_delta = lax.ragged_dot(
        rank_projected, up_factor, group_row_count, preferred_element_type=jnp.float32
    ).astype(jnp.bfloat16)
    adapter_delta = jnp.take(sorted_delta, inverse_order, axis=0).reshape(
        owners, capacity, output_piece
    )
    returned = lax.all_to_all(adapter_delta, "replica", split_axis=0, concat_axis=0, tiled=True)
    adapter_delta_rows = jnp.einsum(
        "pr,po->ro",
        packer,
        returned.reshape(owners * capacity, output_piece),
        preferred_element_type=jnp.float32,
    )
    local_base_output = lax.psum_scatter(partial_base, "tensor", scatter_dimension=1, tiled=True)
    return (local_base_output + ADAPTER_SCALE * adapter_delta_rows).astype(jnp.bfloat16)


def iota(shape, dim):
    return lax.broadcasted_iota(jnp.int32, shape, dim)


def hot(mask):
    return jnp.where(mask, 1.0, 0.0).astype(jnp.bfloat16)


def lookup(request_ref, map_ref, owners, local_adapters):
    rows, adapters = request_ref.shape[1], map_ref.shape[1]
    slots = map_ref[...]
    which = iota((16, adapters), 0)
    owner = lax.div(slots, jnp.int32(local_adapters))
    table = jnp.where(which == 8, slots, jnp.where(which == owner, 1, 0))
    table = table.astype(jnp.float32).astype(jnp.bfloat16)
    one_hot = hot(iota((adapters, rows), 0) == request_ref[...])
    found = jnp.dot(table, one_hot, preferred_element_type=jnp.float32)
    return found[8:9].astype(jnp.int32), found[0:8]


def column_sums(table, counts):
    wide = jnp.broadcast_to(counts, (counts.shape[0], 128)).astype(jnp.bfloat16)
    return jnp.dot(table, wide, preferred_element_type=jnp.float32)[:, :1]


def start_copies(source_ref, target_ref, sems, offset=0):
    size = source_ref.shape[0] // sems.shape[0]
    copies = [
        pltpu.make_async_copy(
            source_ref.at[k * size : (k + 1) * size],
            target_ref.at[offset + k * size : offset + (k + 1) * size],
            sems.at[k],
        )
        for k in range(sems.shape[0])
    ]
    for copy in copies:
        copy.start()
    return copies


def route_kernel(
    owners, local_adapters, me_ref, request_ref, map_ref, tokens_ref,
    first_ref, over_ref, place_ref, branch_ref,
    request_held, map_held, rows_ref, packed_ref, sems, out_sems,
):
    small = [
        pltpu.make_async_copy(source, target, out_sems.at[k])
        for k, (source, target) in enumerate(((request_ref, request_held), (map_ref, map_held)))
    ]
    for copy in small:
        copy.start()
    rows, width = tokens_ref.shape
    capacity = 2 * rows // owners
    half = capacity // 2
    pool = map_ref.shape[1]
    copies = start_copies(tokens_ref, rows_ref, sems)
    me = me_ref[0]
    before = hot(iota((rows, rows), 0) < iota((rows, rows), 1))
    for copy in small:
        copy.wait()
    slots, marks = lookup(request_held, map_held, owners, local_adapters)
    most = jnp.zeros((8, 1), jnp.float32)
    slot = jnp.zeros((1, rows), jnp.int32)
    for source in range(owners):
        span = slice(source * rows, (source + 1) * rows)
        most = jnp.maximum(most, jnp.sum(marks[:, span], axis=1, keepdims=True))
        slot = jnp.where(me == source, slots[:, span], slot)
    over = jnp.where(most > half, 1, 0)
    branch = jnp.where(jnp.sum(over) <= 1, jnp.sum(over * iota((8, 1), 0)), owners)
    branch_ref[0] = branch
    mine = iota((pool, rows), 0) == slot
    one_hot = hot(mine)
    ranks = jnp.dot(one_hot, before, preferred_element_type=jnp.float32)
    counts = jnp.sum(jnp.where(mine, 1.0, 0.0), axis=1, keepdims=True)
    row, column = iota((pool, pool), 0), iota((pool, pool), 1)
    same = lax.div(row, jnp.int32(local_adapters)) == lax.div(column, jnp.int32(local_adapters))
    ranks += column_sums(hot(same & (column < row)), counts)
    rank = jnp.sum(jnp.where(mine, ranks, 0.0), axis=0, keepdims=True).astype(jnp.int32)
    owner = lax.div(slot, jnp.int32(local_adapters))
    place_ref[...] = jnp.broadcast_to(owner * capacity + rank, (8, rows))
    target = jnp.where(branch < owners, branch, me)
    late = jnp.where((owner == target) & (rank >= half), rank - half, -1)
    first = jnp.where(rank < half, owner * half + rank, -1)
    for copy in copies:
        copy.wait()
    sends = []
    for k in range(owners + 1):
        index = late if k == 0 else first - (k - 1) * half
        packer = hot(iota((half, rows), 0) == index)
        packed = jnp.dot(packer, rows_ref[...], preferred_element_type=jnp.float32)
        packed_ref[k * half : (k + 1) * half, :] = packed.astype(jnp.bfloat16)
        target_ref = over_ref if k == 0 else first_ref.at[(k - 1) * half : k * half]
        sends.append(
            pltpu.make_async_copy(packed_ref.at[k * half : (k + 1) * half], target_ref, out_sems.at[k])
        )
        sends[-1].start()
    for send in sends:
        send.wait()


def route(me, requests, slot_map, tokens, owners, local_adapters):
    rows, width = tokens.shape
    half = rows // owners
    vmem, smem = pl.BlockSpec(memory_space=pltpu.VMEM), pl.BlockSpec(memory_space=pltpu.SMEM)
    anywhere = pl.BlockSpec(memory_space=pl.ANY)
    return pl.pallas_call(
        functools.partial(route_kernel, owners, local_adapters),
        in_specs=[smem, anywhere, anywhere, anywhere],
        out_specs=[anywhere, anywhere, vmem, smem],
        out_shape=[
            pltpu.HBM((rows, width), jnp.bfloat16),
            pltpu.HBM((half, width), jnp.bfloat16),
            jax.ShapeDtypeStruct((8, rows), jnp.int32),
            jax.ShapeDtypeStruct((1,), jnp.int32),
        ],
        scratch_shapes=[
            pltpu.VMEM(requests.shape, jnp.int32),
            pltpu.VMEM(slot_map.shape, jnp.int32),
            pltpu.VMEM((rows, width), jnp.bfloat16),
            pltpu.VMEM((rows + half, width), jnp.bfloat16),
            pltpu.SemaphoreType.DMA((COPIES,)),
            pltpu.SemaphoreType.DMA((owners + 1,)),
        ],
        compiler_params=pltpu.CompilerParams(vmem_limit_bytes=VMEM_BYTES),
        name="route",
    )(me, requests, slot_map, tokens)


def plan_kernel(
    owners, local_adapters, rows, me_ref, request_ref, map_ref, adapter_ref, bound_ref
):
    me = me_ref[0]
    capacity = 2 * rows // owners
    slots, _ = lookup(request_ref, map_ref, owners, local_adapters)
    shape = (local_adapters, local_adapters)
    upto = hot(iota(shape, 1) <= iota(shape, 0))
    place = iota((local_adapters, capacity), 1)
    found = []
    for source in range(owners):
        slot = slots[:, source * rows : (source + 1) * rows]
        mine = iota((local_adapters, rows), 0) + me * local_adapters == slot
        counts = jnp.sum(jnp.where(mine, 1.0, 0.0), axis=1, keepdims=True)
        ends = column_sums(upto, counts).astype(jnp.int32)
        passed = jnp.sum(jnp.where(ends <= place, 1, 0), axis=0, keepdims=True)
        found.append(jnp.where(passed < local_adapters, passed, -1))
    size = capacity // GROUPS
    for group in range(GROUPS):
        span = slice(group * size, (group + 1) * size)
        pieces = []
        for k in range(owners):
            if group < GROUPS // 2:
                pieces.append(found[k][:, span])
                continue
            piece = found[0][:, span]
            for source in range(1, owners):
                here = lax.rem(me - k + owners, owners) == source
                piece = jnp.where(here, found[source][:, span], piece)
            pieces.append(piece)
        row = jnp.concatenate(pieces, axis=1)
        adapter_ref[:, group * owners * size : (group + 1) * owners * size] = jnp.broadcast_to(
            row, (8, owners * size)
        )
        bound_ref[2 * group] = jnp.min(jnp.where(row < 0, local_adapters, row))
        bound_ref[2 * group + 1] = jnp.max(row)


def plan(me, requests, slot_map, owners, local_adapters):
    rows = requests.shape[1] // owners
    vmem, smem = pl.BlockSpec(memory_space=pltpu.VMEM), pl.BlockSpec(memory_space=pltpu.SMEM)
    return pl.pallas_call(
        functools.partial(plan_kernel, owners, local_adapters, rows),
        in_specs=[smem, vmem, vmem],
        out_specs=[vmem, smem],
        out_shape=[
            jax.ShapeDtypeStruct((8, 2 * rows), jnp.int32),
            jax.ShapeDtypeStruct((2 * GROUPS,), jnp.int32),
        ],
        compiler_params=pltpu.CompilerParams(vmem_limit_bytes=VMEM_BYTES),
        cost_estimate=BRIEF,
        name="plan",
    )(me, requests, slot_map)


def base_kernel(me_ref, tokens_ref, weight_ref, near_ref, far_ref, give_ref, total_ref):
    total_ref[...] = jnp.dot(tokens_ref[...], weight_ref[...], preferred_element_type=jnp.float32)
    piece = near_ref.shape[1]
    for bit, out_ref in enumerate((near_ref, give_ref.at[0], far_ref, give_ref.at[1])):
        column = pl.multiple_of((me_ref[0] ^ bit) * piece, piece)
        out_ref[...] = total_ref[:, pl.ds(column, piece)]


def base_sum(tokens, weight):
    me = lax.axis_index("tensor").astype(jnp.int32).reshape(1)
    rows, columns = tokens.shape[0], weight.shape[1]
    vmem, smem = pl.BlockSpec(memory_space=pltpu.VMEM), pl.BlockSpec(memory_space=pltpu.SMEM)
    piece = jax.ShapeDtypeStruct((rows, columns // 4), jnp.float32)
    near, far, give = pl.pallas_call(
        base_kernel,
        in_specs=[smem, vmem, vmem],
        out_specs=[vmem] * 3,
        out_shape=[piece, piece, jax.ShapeDtypeStruct((2, *piece.shape), jnp.float32)],
        scratch_shapes=[pltpu.VMEM((rows, columns), jnp.float32)],
        compiler_params=pltpu.CompilerParams(vmem_limit_bytes=VMEM_BYTES),
        cost_estimate=BRIEF,
        name="base",
    )(me, tokens, weight)
    came = exchange(give, "tensor", 1)
    return near + came[0] + exchange(far + came[1], "tensor", 2)


def gather_rows(sent_refs, rows_ref, sems, owners):
    groups = GROUPS // 2
    size = rows_ref.shape[0] // groups
    share = size // owners
    copies = []
    for group in range(groups):
        for k in range(owners):
            if len(sent_refs) == 1:
                at = (groups * k + group) * share
                source = sent_refs[0].at[at : at + share]
            else:
                source = sent_refs[k].at[group * share : (group + 1) * share]
            target = rows_ref.at[group * size + k * share : group * size + (k + 1) * share]
            copies.append(pltpu.make_async_copy(source, target, sems.at[group * owners + k]))
    for copy in copies:
        copy.start()
    return copies


def add_blocks(part, rank, first, last, wait, bound_ref, adapter_ref, held_ref, rows_ref, total_ref):
    groups = GROUPS // 2
    size = rows_ref.shape[0] // groups
    wide = BLOCK * rank

    def block(step, carry):
        wait(step)
        start = step * BLOCK
        for group in range(groups):
            low, high = (bound_ref[2 * (part * groups + group) + k] for k in range(2))

            @pl.when((low < start + BLOCK) & (high >= start))
            def _():
                products = lax.dot_general(
                    held_ref[pl.ds(pl.multiple_of(step * wide, wide), wide), :],
                    rows_ref[group * size : (group + 1) * size, :],
                    NT,
                    preferred_element_type=jnp.float32,
                )
                at = (part * groups + group) * size
                total = total_ref[:, group * size : (group + 1) * size]
                for k in range(BLOCK):
                    chosen = adapter_ref[0:1, at : at + size] == start + k
                    total += jnp.where(chosen, products[k * rank : (k + 1) * rank], 0.0)
                total_ref[:, group * size : (group + 1) * size] = total

        return carry

    lax.fori_loop(first, last, block, 0)


def early_kernel(
    rank, owners, bound_ref, adapter_ref, down_ref, sent_ref,
    total_ref, held_ref, rows_ref, sems, held_sems,
):
    blocks = held_sems.shape[0]
    copies = gather_rows([sent_ref], rows_ref, sems, owners)
    fetches = start_copies(down_ref, held_ref, held_sems)
    total_ref[...] = jnp.zeros_like(total_ref)
    for copy in copies:
        copy.wait()

    def wait(step):
        at = pl.ds(pl.multiple_of(step * BLOCK * rank, BLOCK * rank), BLOCK * rank)
        pltpu.make_async_copy(down_ref.at[at], held_ref.at[at], held_sems.at[step]).wait()

    add_blocks(0, rank, 0, blocks, wait, bound_ref, adapter_ref, held_ref, rows_ref, total_ref)


def early_down(bounds, adapter_row, down_rows, sent, rank, owners):
    height, width = down_rows.shape
    slots = adapter_row.shape[1] // 2
    vmem, anywhere = pl.BlockSpec(memory_space=pltpu.VMEM), pl.BlockSpec(memory_space=pl.ANY)
    return pl.pallas_call(
        functools.partial(early_kernel, rank, owners),
        in_specs=[pl.BlockSpec(memory_space=pltpu.SMEM), vmem, anywhere, anywhere],
        out_specs=[vmem, vmem],
        out_shape=[
            jax.ShapeDtypeStruct((rank, slots), jnp.float32),
            pltpu.VMEM((height, width), jnp.bfloat16),
        ],
        scratch_shapes=[
            pltpu.VMEM((slots, width), jnp.bfloat16),
            pltpu.SemaphoreType.DMA((GROUPS // 2 * owners,)),
            pltpu.SemaphoreType.DMA((height // (BLOCK * rank),)),
        ],
        compiler_params=pltpu.CompilerParams(vmem_limit_bytes=VMEM_BYTES),
        cost_estimate=BRIEF,
        name="early_down",
    )(bounds, adapter_row, pltpu.with_memory_space_constraint(down_rows, pltpu.HBM), sent)


def late_kernel(rank, owners, *refs):
    bound_ref, side_ref, adapter_ref, held_ref, early_ref = refs[:5]
    sent_refs = refs[5 : 5 + owners]
    keep_ref, give_ref, rows_ref, total_ref, sems = refs[5 + owners :]
    copies = gather_rows(sent_refs, rows_ref, sems, owners)
    groups = GROUPS // 2
    size = rows_ref.shape[0] // groups
    wide = BLOCK * rank
    pool = held_ref.shape[0] // rank
    total_ref[...] = jnp.zeros_like(total_ref)
    for group in range(groups):
        low, high = (bound_ref[2 * (groups + group) + k] for k in range(2))
        span = slice(group * size, (group + 1) * size)
        at = (groups + group) * size
        for copy in copies[group * owners : (group + 1) * owners]:
            copy.wait()

        def block(step, carry):
            fresh = low + step * BLOCK
            start = jnp.minimum(fresh, pool - BLOCK)
            products = lax.dot_general(
                held_ref[pl.ds(pl.multiple_of(start * rank, rank), wide), :],
                rows_ref[span, :],
                NT,
                preferred_element_type=jnp.float32,
            )
            adapter = adapter_ref[0:1, at : at + size]
            adapter = jnp.where(adapter < fresh, -1, adapter - start)
            total = total_ref[:, span]
            for k in range(BLOCK):
                total += jnp.where(adapter == k, products[k * rank : (k + 1) * rank], 0.0)
            total_ref[:, span] = total
            return carry

        lax.fori_loop(0, lax.div(high - low + BLOCK, jnp.int32(BLOCK)), block, 0)
    side = side_ref[0]
    one, two = early_ref[...], total_ref[...]
    keep_ref[...] = jnp.where(side == 0, one, two)
    give_ref[...] = jnp.where(side == 0, two, one)


def late_down(bounds, side, adapter_row, held, early, sent, rank, owners):
    width = held.shape[1]
    vmem, smem = pl.BlockSpec(memory_space=pltpu.VMEM), pl.BlockSpec(memory_space=pltpu.SMEM)
    return pl.pallas_call(
        functools.partial(late_kernel, rank, owners),
        in_specs=[smem, smem, vmem, vmem, vmem] + [pl.BlockSpec(memory_space=pl.ANY)] * owners,
        out_specs=[vmem, vmem],
        out_shape=[jax.ShapeDtypeStruct(early.shape, jnp.float32)] * 2,
        scratch_shapes=[
            pltpu.VMEM((early.shape[1], width), jnp.bfloat16),
            pltpu.VMEM(early.shape, jnp.float32),
            pltpu.SemaphoreType.DMA((GROUPS // 2 * owners,)),
        ],
        compiler_params=pltpu.CompilerParams(vmem_limit_bytes=VMEM_BYTES),
        cost_estimate=BRIEF,
        name="late_down",
    )(bounds, side, adapter_row, pltpu.with_memory_space_constraint(held, pltpu.VMEM), early, *sent)


def up_kernel(owners, rank, adapters, me_ref, side_ref, adapter_ref, up_ref, mine_ref, other_ref, *refs):
    out_refs, held_ref = refs[:-1], refs[-1]
    me, side = me_ref[0], side_ref[0]
    mine, other = mine_ref[...].astype(jnp.float32), other_ref[...].astype(jnp.float32)
    groups = GROUPS // 2
    size = mine.shape[1] // groups
    share = size // owners
    for group in range(GROUPS):
        part, inner = group // groups, group % groups
        span = slice(inner * size, (inner + 1) * size)
        low_rank = jnp.where(side == part, mine[:, span], other[:, span])
        chosen = adapter_ref[0:1, group * size : (group + 1) * size]
        spread = jnp.concatenate(
            [jnp.where(chosen == k, low_rank, 0.0).astype(jnp.bfloat16) for k in range(adapters)],
            axis=0,
        )
        delta = lax.dot_general(up_ref[...], spread, TN, preferred_element_type=jnp.float32)
        delta = delta.astype(jnp.bfloat16)
        for k in range(owners):
            source = (k if part == 0 else lax.rem(me - k + owners, owners)) ^ me
            held_ref[source, :, group * share : (group + 1) * share] = delta[:, k * share : (k + 1) * share]
    for bit, out_ref in enumerate(out_refs):
        out_ref[...] = held_ref[bit]


def up(me, side, adapter_row, up_rows, mine, other, owners):
    rank, wide = mine.shape
    piece = up_rows.shape[1]
    adapters = up_rows.shape[0] // rank
    vmem, smem = pl.BlockSpec(memory_space=pltpu.VMEM), pl.BlockSpec(memory_space=pltpu.SMEM)
    return pl.pallas_call(
        functools.partial(up_kernel, owners, rank, adapters),
        in_specs=[smem, smem, vmem, vmem, vmem, vmem],
        out_shape=[jax.ShapeDtypeStruct((piece, 2 * wide // owners), jnp.bfloat16)] * owners,
        scratch_shapes=[pltpu.VMEM((owners, piece, 2 * wide // owners), jnp.bfloat16)],
        compiler_params=pltpu.CompilerParams(vmem_limit_bytes=VMEM_BYTES),
        cost_estimate=BRIEF,
        name="up",
    )(me, side, adapter_row, up_rows, mine, other)


def tensor_sum(keep, give):
    keep = keep + exchange(give, "tensor", 1)
    keep = keep + exchange(keep, "tensor", 2)
    mine = keep.astype(jnp.bfloat16)
    return mine, exchange(mine, "tensor", 1)


def unpack_kernel(owners, me_ref, place_ref, *refs):
    returned_refs, base_ref, out_ref, held_ref, sem = refs[:owners], *refs[owners:]
    copy = pltpu.make_async_copy(base_ref, held_ref, sem)
    copy.start()
    rows = out_ref.shape[0]
    features, capacity = returned_refs[0].shape
    total = jnp.zeros((features, rows), jnp.float32)
    for bit in range(owners):
        spot = place_ref[0:1, :] - (me_ref[0] ^ bit) * capacity
        selector = hot(iota((capacity, rows), 0) == spot)
        total += jnp.dot(returned_refs[bit][...], selector, preferred_element_type=jnp.float32)
    copy.wait()
    out_ref[...] = (held_ref[...] + ADAPTER_SCALE * total.T).astype(jnp.bfloat16)


def unpack(me, place, returned, base):
    vmem, smem = pl.BlockSpec(memory_space=pltpu.VMEM), pl.BlockSpec(memory_space=pltpu.SMEM)
    return pl.pallas_call(
        functools.partial(unpack_kernel, len(returned)),
        in_specs=[smem, vmem] + [vmem] * len(returned) + [pl.BlockSpec(memory_space=pl.ANY)],
        out_specs=vmem,
        out_shape=pltpu.HBM(base.shape, jnp.bfloat16),
        scratch_shapes=[pltpu.VMEM(base.shape, jnp.float32), pltpu.SemaphoreType.DMA],
        compiler_params=pltpu.CompilerParams(vmem_limit_bytes=VMEM_BYTES),
        cost_estimate=BRIEF,
        name="unpack",
    )(me, place, *returned, base)


def exchange(array, axis, bit):
    size = lax.axis_size(axis)
    return lax.ppermute(array, axis, [(k, k ^ bit) for k in range(size)])


def swap(array):
    return lax.all_to_all(array, "replica", split_axis=0, concat_axis=0, tiled=True)


def body(tokens, value_weight, down_factor, up_factor, request_adapter, adapter_slot_map):
    row_count, quarter = tokens.shape
    owners = lax.axis_size("replica")
    local_adapters, _, rank = down_factor.shape
    half = row_count // owners
    me = lax.axis_index("replica").astype(jnp.int32).reshape(1)
    side = (lax.axis_index("tensor").astype(jnp.int32) % 2).reshape(1)
    requests = request_adapter.reshape(1, -1)
    slot_map = adapter_slot_map.reshape(1, -1)
    down_rows = jnp.swapaxes(down_factor, 1, 2).reshape(local_adapters * rank, quarter)
    up_rows = up_factor.reshape(local_adapters * rank, -1)

    first, over, place, branch = route(me, requests, slot_map, tokens, owners, local_adapters)

    def work(late, place, first, over, tokens, value_weight, down_rows, up_rows, requests, slot_map):
        arrived = swap(first.reshape(owners, half, quarter)).reshape(owners * half, quarter)
        base = base_sum(tokens, value_weight)
        adapter_row, bounds = plan(me, requests, slot_map, owners, local_adapters)
        adapter_row, base = lax.optimization_barrier((adapter_row, base))
        early, held = early_down(bounds, adapter_row, down_rows, arrived, rank, owners)
        keep, give = late_down(bounds, side, adapter_row, held, early, (over, *late), rank, owners)
        mine, other = tensor_sum(keep, give)
        delta = up(me, side, adapter_row, up_rows, mine, other, owners)
        returned = [delta[0]] + [exchange(delta[bit], "replica", bit) for bit in range(1, owners)]
        return unpack(me, place, returned, base)

    def to_one(owner):
        def send(place, first, over, tokens, *rest):
            late = tuple(
                lax.ppermute(over, "replica", [((owner - shift) % owners, owner)])
                for shift in range(1, owners)
            )
            return work(late, place, first, over, tokens, *rest)

        return send

    def to_all(place, first, over, tokens, *rest):
        spot = place[0]
        owner, late = spot // (2 * half), spot % (2 * half) - half
        index = jnp.where(late >= 0, owner * half + late, -1)
        packer = (jnp.arange(owners * half)[:, None] == index[None, :]).astype(jnp.bfloat16)
        outgoing = jnp.dot(packer, tokens, preferred_element_type=jnp.float32)
        outgoing = outgoing.astype(jnp.bfloat16).reshape(owners, half, quarter)
        came = lax.all_to_all(outgoing, "replica", split_axis=0, concat_axis=0, tiled=True)
        here = lax.axis_index("replica")
        late = tuple(
            lax.dynamic_index_in_dim(came, (here - shift) % owners, 0, keepdims=False)
            for shift in range(1, owners)
        )
        return work(late, place, first, over, tokens, *rest)

    return lax.switch(
        branch[0],
        [to_one(owner) for owner in range(owners)] + [to_all],
        place, first, over, tokens, value_weight, down_rows, up_rows, requests, slot_map,
    )


def solution(mesh):
    in_specs = (
        P(("parts", "replica"), "tensor"),
        P("tensor", None),
        P(("parts", "replica"), "tensor", None),
        P(("parts", "replica"), None, "tensor"),
        P("parts"),
        P("parts"),
    )
    out_specs = P(("parts", "replica"), "tensor")
    small = mesh.shape["replica"] <= MAX_OWNERS and mesh.shape["tensor"] == 4
    chosen = body if small else plain_body
    return jax.shard_map(chosen, mesh=mesh, in_specs=in_specs, out_specs=out_specs, check_vma=False)
```

profile of v0, /device:TPU:0, one launch (start us, length us, event | category | flops | bytes accessed | tf_op | source)
XLA Modules:
  0.0 106.0 jit_solution(5444171445880659943)
XLA Ops:
  0.0 0.0 copy-start.8
  0.0 0.0 copy-start.7
  0.0 4.9 %route.1 = (bf16[512,2048]{1,0:T(8,128)(2,1)}, bf16[128,2048]{1,0:T(8,128)(2,1)}, s32[8,512]{1,0:T(8,128)S(1)}, s32[1]{0:T(128)}) custom-call(s32[1]{0:T(128)} %bitcast.30.me_ref, s32[1,2048]{1,0:T(1,128)} %bitcast.104, s32[1,128]{1,0:T(1,128)} %bitcast.110, bf16[512,2048]{1,0:T(8,128)(2,1)} %tokens_ref.1), custom_call_target="tpu_custom_call" | custom-call | tf_op jit(solution)/shard_map/route/pallas_call | solution.py:178
  5.6 0.0 copy-done.8
  5.6 0.0 copy-done.7
  5.6 100.1 %conditional.1 = (bf16[512,128]{1,0:T(8,128)(2,1)}) conditional(s32[]{:T(128)} %bitcast.33, (s32[1]{0:T(128)}, s32[1,2048]{1,0:T(1,128)S(1)}, s32[1,128]{1,0:T(1,128)S(1)}, bf16[512,2048]{1,0:T(8,128)(2,1)}, bf16[2048,512]{1,0:T(8,128)(2,1)}, /*index=5*/bf16[512,2048]{1,0:T(8,128)(2,1)}, ...), branch_computations={%region_0.1_spmd, %region_1.2_spmd, %region_2.3_spmd, %region_3.4_... | conditional | flops 1075359744 | bytes 96934912 | solution.py:571
  5.8 6.3 %all-to-all-start.2 = ((bf16[4,128,2048]{2,1,0:T(8,128)(2,1)}), bf16[4,128,2048]{2,1,0:T(8,128)(2,1)S(1)}, u32[]{:S(2)}, u32[]{:S(2)}) async-start(bf16[4,128,2048]{2,1,0:T(8,128)(2,1)} %bitcast.95), calls=%async_computation.2 | async-start | bytes 4194304 | tf_op jit(solution)/shard_map/cond/branch_2_fun/all_to_all | solution.py:517
  12.2 3.6 %base.7 = (f32[512,128]{1,0:T(8,128)S(1)}, f32[512,128]{1,0:T(8,128)S(1)}, f32[2,512,128]{2,1,0:T(8,128)S(1)}) custom-call(s32[1]{0:T(128)} %bitcast.10.me_ref, bf16[512,2048]{1,0:T(8,128)(2,1)} %get-tuple-element.179.tokens_ref, bf16[2048,512]{1,0:T(8,128)(2,1)} %get-tuple-element.180.weight_ref), custom_call_target="tpu_custom_call" | custom-call | tf_op jit(solution)/shard_map/cond/branch_2_fun/base/pallas_call | solution.py:269
  15.8 0.1 collective-permute-start.22
  15.8 0.7 collective-permute-start.26
  16.5 5.5 %collective-permute-start.25 = (bf16[128,2048]{1,0:T(8,128)(2,1)}, bf16[128,2048]{1,0:T(8,128)(2,1)S(1)}, u32[]{:S(2)}, u32[]{:S(2)}) collective-permute-start(bf16[128,2048]{1,0:T(8,128)(2,1)} %get-tuple-element.191.refs_5_), channel_id=1, source_target_pairs={{0,8},{1,9},{2,10},{3,11},{16,24},{17,25},{18,26},{19,27}} | collective-permute-start | bytes 1572872 | tf_op jit(solution)/shard_map/cond/branch_2_fun/ppermute | solution.py:549
  22.0 1.5 %collective-permute-start.24 = (bf16[128,2048]{1,0:T(8,128)(2,1)}, bf16[128,2048]{1,0:T(8,128)(2,1)}, u32[]{:S(2)}, u32[]{:S(2)}) collective-permute-start(bf16[128,2048]{1,0:T(8,128)(2,1)} %get-tuple-element.191.refs_5_), channel_id=1, source_target_pairs={{4,8},{5,9},{6,10},{7,11},{20,24},{21,25},{22,26},{23,27}} | collective-permute-start | bytes 1572872 | tf_op jit(solution)/shard_map/cond/branch_2_fun/ppermute | solution.py:549
  23.5 0.0 collective-permute-done.22
  23.5 1.6 %collective-permute-start.23 = (f32[512,128]{1,0:T(8,128)S(1)}, f32[512,128]{1,0:T(8,128)S(1)}, u32[]{:S(2)}, u32[]{:S(2)}) collective-permute-start(f32[512,128]{1,0:T(8,128)S(1)} %fusion.6), channel_id=1, source_target_pairs={{0,2},{1,3},{2,0},{3,1},{4,6},{5,7},{6,4},{7,5},{8,10},{9,11},{10,... | collective-permute-start | bytes 786440 | tf_op jit(solution)/shard_map/cond/branch_2_fun/ppermute | solution.py:513
  25.1 1.3 %plan.7 = (s32[8,1024]{1,0:T(8,128)S(1)}, s32[8]{0:T(128)S(1)}) custom-call(s32[1]{0:T(128)} %get-tuple-element.173.me_ref, s32[1,2048]{1,0:T(1,128)S(1)} %get-tuple-element.176.request_ref, s32[1,128]{1,0:T(1,128)S(1)} %get-tuple-element.177.map_ref), custom_call_target="tpu_custom_call" | custom-call | tf_op jit(solution)/shard_map/cond/branch_2_fun/plan/pallas_call | solution.py:242
  26.4 5.6 %collective-permute-done.23 = f32[512,128]{1,0:T(8,128)S(1)} collective-permute-done((f32[512,128]{1,0:T(8,128)S(1)}, f32[512,128]{1,0:T(8,128)S(1)}, u32[]{:S(2)}, u32[]{:S(2)}) %collective-permute-start.23) | collective-permute-done | bytes 262176 | tf_op jit(solution)/shard_map/cond/branch_2_fun/ppermute | solution.py:513
  32.0 28.3 %all-to-all-done.2 = bf16[4,128,2048]{2,1,0:T(8,128)(2,1)S(1)} async-done(((bf16[4,128,2048]{2,1,0:T(8,128)(2,1)}), bf16[4,128,2048]{2,1,0:T(8,128)(2,1)S(1)}, u32[]{:S(2)}, u32[]{:S(2)}) %all-to-all-start.2) | async-done | bytes 2097184 | tf_op jit(solution)/shard_map/cond/branch_2_fun/all_to_all | solution.py:517
  60.4 7.8 %early_down.7 = (f32[64,512]{1,0:T(8,128)S(1)}, bf16[2048,2048]{1,0:T(8,128)(2,1)S(1)}) custom-call(s32[8]{0:T(128)S(1)} %get-tuple-element.186.bound_ref.refs_0_, s32[8,1024]{1,0:T(8,128)S(1)} %get-tuple-element.184.adapter_ref.refs_2_, bf16[2048,2048]{1,0:T(8,128)(2,1)} %get-tuple-element.187.down_ref, bf16[512,2048]{1,0:T(8,128)(2,1)S(1)} %bitcast.86), custom_call_target="tpu_custom_call" | custom-call | tf_op jit(solution)/shard_map/cond/branch_2_fun/early_down/pallas_call | solution.py:355
  68.2 0.0 collective-permute-done.26.refs_8_
  68.2 0.0 collective-permute-done.25.refs_7_
  68.2 0.0 collective-permute-done.24.refs_6_
  68.2 0.0 copy-start.4
  68.2 1.8 %late_down.7 = (f32[64,512]{1,0:T(8,128)S(1)}, f32[64,512]{1,0:T(8,128)S(1)}) custom-call(s32[8]{0:T(128)S(1)} %get-tuple-element.186.bound_ref.refs_0_, s32[1]{0:T(128)} %get-tuple-element.175.refs_1_.side_ref, s32[8,1024]{1,0:T(8,128)S(1)} %get-tuple-element.184.adapter_ref.refs_2_, bf16[2048,2048]{1,0:T(8,128)(2,1)S(1)} %get-tuple-element.189.refs_3_, ...), custom_call_target="tpu_custom_call" | custom-call | tf_op jit(solution)/shard_map/cond/branch_2_fun/late_down/pallas_call | solution.py:418
  70.1 0.1 collective-permute-start.27
  70.1 1.3 %collective-permute-done.27 = f32[64,512]{1,0:T(8,128)S(1)} collective-permute-done((f32[64,512]{1,0:T(8,128)S(1)}, f32[64,512]{1,0:T(8,128)S(1)}, u32[]{:S(2)}, u32[]{:S(2)}) %collective-permute-start.27) | collective-permute-done | bytes 131104 | tf_op jit(solution)/shard_map/cond/branch_2_fun/ppermute | solution.py:513
  71.5 1.6 %collective-permute-start.28 = (f32[64,512]{1,0:T(8,128)S(1)}, f32[64,512]{1,0:T(8,128)S(1)}, u32[]{:S(2)}, u32[]{:S(2)}) collective-permute-start(f32[64,512]{1,0:T(8,128)S(1)} %add.95), channel_id=1, source_target_pairs={{0,2},{1,3},{2,0},{3,1},{4,6},{5,7},{6,4},{7,5},{8,10},{9,11},{10,... | collective-permute-start | bytes 393224 | tf_op jit(solution)/shard_map/cond/branch_2_fun/ppermute | solution.py:513
  73.1 4.1 %collective-permute-done.28 = f32[64,512]{1,0:T(8,128)S(1)} collective-permute-done((f32[64,512]{1,0:T(8,128)S(1)}, f32[64,512]{1,0:T(8,128)S(1)}, u32[]{:S(2)}, u32[]{:S(2)}) %collective-permute-start.28) | collective-permute-done | bytes 131104 | tf_op jit(solution)/shard_map/cond/branch_2_fun/ppermute | solution.py:513
  77.1 0.1 collective-permute-start.29
  77.2 1.2 %collective-permute-done.29.other_ref = bf16[64,512]{1,0:T(8,128)(2,1)S(1)} collective-permute-done((bf16[64,512]{1,0:T(8,128)(2,1)S(1)}, bf16[64,512]{1,0:T(8,128)(2,1)S(1)}, u32[]{:S(2)}, u32[]{:S(2)}) %collective-permute-start.29) | collective-permute-done | bytes 65568 | tf_op jit(solution)/shard_map/cond/branch_2_fun/ppermute | solution.py:513
  78.5 0.0 copy-done.4
  78.5 0.9 up.7
  79.4 13.4 %collective-permute-start.30 = (bf16[128,256]{1,0:T(8,128)(2,1)S(1)}, bf16[128,256]{1,0:T(8,128)(2,1)S(1)}, u32[]{:S(2)}, u32[]{:S(2)}) collective-permute-start(bf16[128,256]{1,0:T(8,128)(2,1)S(1)} %get-tuple-element.195), channel_id=1, source_target_pairs={{0,4},{4,0},{8,12},{12,8},{1,5},{5,1},{9,13},{13,9},{2,6},{6,2},{1... | collective-permute-start | bytes 196616 | tf_op jit(solution)/shard_map/cond/branch_2_fun/ppermute | solution.py:513
  92.8 5.1 %collective-permute-start.31 = (bf16[128,256]{1,0:T(8,128)(2,1)S(1)}, bf16[128,256]{1,0:T(8,128)(2,1)S(1)}, u32[]{:S(2)}, u32[]{:S(2)}) collective-permute-start(bf16[128,256]{1,0:T(8,128)(2,1)S(1)} %get-tuple-element.196), channel_id=1, source_target_pairs={{0,8},{4,12},{8,0},{12,4},{1,9},{5,13},{9,1},{13,5},{2,10},{6,14},... | collective-permute-start | bytes 196616 | tf_op jit(solution)/shard_map/cond/branch_2_fun/ppermute | solution.py:513
  97.9 1.4 %collective-permute-start.32 = (bf16[128,256]{1,0:T(8,128)(2,1)S(1)}, bf16[128,256]{1,0:T(8,128)(2,1)S(1)}, u32[]{:S(2)}, u32[]{:S(2)}) collective-permute-start(bf16[128,256]{1,0:T(8,128)(2,1)S(1)} %get-tuple-element.197), channel_id=1, source_target_pairs={{0,12},{4,8},{8,4},{12,0},{1,13},{5,9},{9,5},{13,1},{2,14},{6,10},... | collective-permute-start | bytes 196616 | tf_op jit(solution)/shard_map/cond/branch_2_fun/ppermute | solution.py:513
  99.3 0.0 collective-permute-done.30.refs_1_
  99.3 1.0 collective-permute-done.31.refs_2_
  100.3 4.0 %collective-permute-done.32.refs_3_ = bf16[128,256]{1,0:T(8,128)(2,1)S(1)} collective-permute-done((bf16[128,256]{1,0:T(8,128)(2,1)S(1)}, bf16[128,256]{1,0:T(8,128)(2,1)S(1)}, u32[]{:S(2)}, u32[]{:S(2)}) %collective-permute-start.32) | collective-permute-done | bytes 65568 | tf_op jit(solution)/shard_map/cond/branch_2_fun/ppermute | solution.py:513
  104.4 1.1 %unpack.7 = bf16[512,128]{1,0:T(8,128)(2,1)} custom-call(s32[1]{0:T(128)} %get-tuple-element.173.me_ref, s32[8,512]{1,0:T(8,128)S(1)} %get-tuple-element.174.place_ref, bf16[128,256]{1,0:T(8,128)(2,1)S(1)} %get-tuple-element.194.refs_0_, bf16[128,256]{1,0:T(8,128)(2,1)S(1)} %collective-permute-done.30.refs_1_, ...), custom_call_target="tpu_custom_call" | custom-call | tf_op jit(solution)/shard_map/cond/branch_2_fun/unpack/pallas_call | solution.py:499
  (4 shorter events, 0.1 us)
Async XLA Ops:
  0.0 5.6 %copy-start.8 = (s32[128]{0:T(128)S(1)}, s32[128]{0:T(128)}, u32[]{:S(2)}) copy-start(s32[128]{0:T(128)} %param.16) | copy-start | bytes 1540
  0.0 5.6 %copy-start.7 = (s32[2048]{0:T(1024)S(1)}, s32[2048]{0:T(1024)}, u32[]{:S(2)}) copy-start(s32[2048]{0:T(1024)} %param.15) | copy-start | bytes 24580
  5.8 54.5 %all-to-all-start.2 = ((bf16[4,128,2048]{2,1,0:T(8,128)(2,1)}), bf16[4,128,2048]{2,1,0:T(8,128)(2,1)S(1)}, u32[]{:S(2)}, u32[]{:S(2)}) async-start(bf16[4,128,2048]{2,1,0:T(8,128)(2,1)} %bitcast.95), calls=%async_computation.2 | async-start | bytes 4194304 | tf_op jit(solution)/shard_map/cond/branch_2_fun/all_to_all | solution.py:517
  15.8 7.7 %collective-permute-start.22 = (f32[2,512,128]{2,1,0:T(8,128)S(1)}, f32[2,512,128]{2,1,0:T(8,128)S(1)}, u32[]{:S(2)}, u32[]{:S(2)}) collective-permute-start(f32[2,512,128]{2,1,0:T(8,128)S(1)} %get-tuple-element.182), channel_id=1, source_target_pairs={{0,1},{1,0},{2,3},{3,2},{4,5},{5,4},{6,7},{7,6},{8,9},{9,8},{10,11... | collective-permute-start | bytes 1572872 | tf_op jit(solution)/shard_map/cond/branch_2_fun/ppermute | solution.py:513
  15.8 52.3 %collective-permute-start.26 = (bf16[128,2048]{1,0:T(8,128)(2,1)}, bf16[128,2048]{1,0:T(8,128)(2,1)S(1)}, u32[]{:S(2)}, u32[]{:S(2)}) collective-permute-start(bf16[128,2048]{1,0:T(8,128)(2,1)} %get-tuple-element.191.refs_5_), channel_id=1, source_target_pairs={{12,8},{13,9},{14,10},{15,11},{28,24},{29,25},{30,26},{31,27}} | collective-permute-start | bytes 1572872 | tf_op jit(solution)/shard_map/cond/branch_2_fun/ppermute | solution.py:549
  16.5 51.6 %collective-permute-start.25 = (bf16[128,2048]{1,0:T(8,128)(2,1)}, bf16[128,2048]{1,0:T(8,128)(2,1)S(1)}, u32[]{:S(2)}, u32[]{:S(2)}) collective-permute-start(bf16[128,2048]{1,0:T(8,128)(2,1)} %get-tuple-element.191.refs_5_), channel_id=1, source_target_pairs={{0,8},{1,9},{2,10},{3,11},{16,24},{17,25},{18,26},{19,27}} | collective-permute-start | bytes 1572872 | tf_op jit(solution)/shard_map/cond/branch_2_fun/ppermute | solution.py:549
  22.0 46.2 %collective-permute-start.24 = (bf16[128,2048]{1,0:T(8,128)(2,1)}, bf16[128,2048]{1,0:T(8,128)(2,1)}, u32[]{:S(2)}, u32[]{:S(2)}) collective-permute-start(bf16[128,2048]{1,0:T(8,128)(2,1)} %get-tuple-element.191.refs_5_), channel_id=1, source_target_pairs={{4,8},{5,9},{6,10},{7,11},{20,24},{21,25},{22,26},{23,27}} | collective-permute-start | bytes 1572872 | tf_op jit(solution)/shard_map/cond/branch_2_fun/ppermute | solution.py:549
  23.5 8.5 %collective-permute-start.23 = (f32[512,128]{1,0:T(8,128)S(1)}, f32[512,128]{1,0:T(8,128)S(1)}, u32[]{:S(2)}, u32[]{:S(2)}) collective-permute-start(f32[512,128]{1,0:T(8,128)S(1)} %fusion.6), channel_id=1, source_target_pairs={{0,2},{1,3},{2,0},{3,1},{4,6},{5,7},{6,4},{7,5},{8,10},{9,11},{10,... | collective-permute-start | bytes 786440 | tf_op jit(solution)/shard_map/cond/branch_2_fun/ppermute | solution.py:513
  68.2 10.3 %copy-start.4 = (bf16[2048,128]{1,0:T(8,128)(2,1)S(1)}, bf16[2048,128]{1,0:T(8,128)(2,1)}, u32[]{:S(2)}) copy-start(bf16[2048,128]{1,0:T(8,128)(2,1)} %get-tuple-element.185.up_ref) | copy-start | bytes 1572868 | tf_op jit(solution)/shard_map/cond
  70.1 1.4 %collective-permute-start.27 = (f32[64,512]{1,0:T(8,128)S(1)}, f32[64,512]{1,0:T(8,128)S(1)}, u32[]{:S(2)}, u32[]{:S(2)}) collective-permute-start(f32[64,512]{1,0:T(8,128)S(1)} %get-tuple-element.193), channel_id=1, source_target_pairs={{0,1},{1,0},{2,3},{3,2},{4,5},{5,4},{6,7},{7,6},{8,9},{9,8},{10,11... | collective-permute-start | bytes 393224 | tf_op jit(solution)/shard_map/cond/branch_2_fun/ppermute | solution.py:513
  71.5 5.6 %collective-permute-start.28 = (f32[64,512]{1,0:T(8,128)S(1)}, f32[64,512]{1,0:T(8,128)S(1)}, u32[]{:S(2)}, u32[]{:S(2)}) collective-permute-start(f32[64,512]{1,0:T(8,128)S(1)} %add.95), channel_id=1, source_target_pairs={{0,2},{1,3},{2,0},{3,1},{4,6},{5,7},{6,4},{7,5},{8,10},{9,11},{10,... | collective-permute-start | bytes 393224 | tf_op jit(solution)/shard_map/cond/branch_2_fun/ppermute | solution.py:513
  77.1 1.3 %collective-permute-start.29 = (bf16[64,512]{1,0:T(8,128)(2,1)S(1)}, bf16[64,512]{1,0:T(8,128)(2,1)S(1)}, u32[]{:S(2)}, u32[]{:S(2)}) collective-permute-start(bf16[64,512]{1,0:T(8,128)(2,1)S(1)} %add_convert_fusion.2.mine_ref), channel_id=1, source_target_pairs={{0,1},{1,0},{2,3},{3,2},{4,5},{5,4},{6,7},{7,6},{8,9},{9,8},{10,11... | collective-permute-start | bytes 196616 | tf_op jit(solution)/shard_map/cond/branch_2_fun/ppermute | solution.py:513
  79.4 20.0 %collective-permute-start.30 = (bf16[128,256]{1,0:T(8,128)(2,1)S(1)}, bf16[128,256]{1,0:T(8,128)(2,1)S(1)}, u32[]{:S(2)}, u32[]{:S(2)}) collective-permute-start(bf16[128,256]{1,0:T(8,128)(2,1)S(1)} %get-tuple-element.195), channel_id=1, source_target_pairs={{0,4},{4,0},{8,12},{12,8},{1,5},{5,1},{9,13},{13,9},{2,6},{6,2},{1... | collective-permute-start | bytes 196616 | tf_op jit(solution)/shard_map/cond/branch_2_fun/ppermute | solution.py:513
  92.8 7.6 %collective-permute-start.31 = (bf16[128,256]{1,0:T(8,128)(2,1)S(1)}, bf16[128,256]{1,0:T(8,128)(2,1)S(1)}, u32[]{:S(2)}, u32[]{:S(2)}) collective-permute-start(bf16[128,256]{1,0:T(8,128)(2,1)S(1)} %get-tuple-element.196), channel_id=1, source_target_pairs={{0,8},{4,12},{8,0},{12,4},{1,9},{5,13},{9,1},{13,5},{2,10},{6,14},... | collective-permute-start | bytes 196616 | tf_op jit(solution)/shard_map/cond/branch_2_fun/ppermute | solution.py:513
  97.9 6.4 %collective-permute-start.32 = (bf16[128,256]{1,0:T(8,128)(2,1)S(1)}, bf16[128,256]{1,0:T(8,128)(2,1)S(1)}, u32[]{:S(2)}, u32[]{:S(2)}) collective-permute-start(bf16[128,256]{1,0:T(8,128)(2,1)S(1)} %get-tuple-element.197), channel_id=1, source_target_pairs={{0,12},{4,8},{8,4},{12,0},{1,13},{5,9},{9,5},{13,1},{2,14},{6,10},... | collective-permute-start | bytes 196616 | tf_op jit(solution)/shard_map/cond/branch_2_fun/ppermute | solution.py:513
where the time goes:
time: 107 us; the launch traced here: 106 us
  waiting for transfers between devices  45.6 us (43%)
  starting transfers between devices  37.2 us (35%)
  Pallas kernels  21.6 us (20%)
    all_to_all x1, waiting for transfers between devices, swap(): lax.all_to_all(array, 'replica', split_axis=0, concat_axis=0, tiled=True)  28.3 us
    ppermute x8, starting transfers between devices, exchange(): return lax.ppermute(array, axis, [(k, k ^ bit) for k in range(size)])  23.3 us
    ppermute x8, waiting for transfers between devices, exchange(): return lax.ppermute(array, axis, [(k, k ^ bit) for k in range(size)])  17.2 us
    pallas_call x1, Pallas kernels, early_down(): pl.pallas_call(functools.partial(early_kernel, rank, owners), in_specs=[p...  7.81 us
    ppermute x3, starting transfers between devices, send(): lax.ppermute(over, 'replica', [((owner - shift) % owners, owner)])  7.62 us
    all_to_all x1, starting transfers between devices, swap(): lax.all_to_all(array, 'replica', split_axis=0, concat_axis=0, tiled=True)  6.32 us
    pallas_call x1, Pallas kernels, route(): pl.pallas_call(functools.partial(route_kernel, owners, local_adapters), i...  4.95 us
    pallas_call x1, Pallas kernels, base_sum(): pl.pallas_call(base_kernel, in_specs=[smem, vmem, vmem], out_specs=[vmem]...  3.6 us
  transfers between devices with their start and end apart: 12, of which 7 were waited for; matrix products, arithmetic and copies ran while one was open for 0% of the time, Pallas kernels for 12%

commit v1 on v0

--- a/solution.py
+++ b/solution.py
@@ -8,7 +8,6 @@
 from jax.sharding import PartitionSpec as P
 
 ADAPTER_SCALE = 0.5
-MAX_OWNERS = 8
 COPIES = 8
 GROUPS = 4
 BLOCK = 4
@@ -479,6 +478,10 @@
     return mine, exchange(mine, "tensor", 1)
 
 
+def return_order(owners):
+    return [*range(2, owners), 1, 0]
+
+
 def unpack_kernel(owners, me_ref, place_ref, *refs):
     returned_refs, base_ref, out_ref, held_ref, sem = refs[:owners], *refs[owners:]
     copy = pltpu.make_async_copy(base_ref, held_ref, sem)
@@ -486,10 +489,10 @@
     rows = out_ref.shape[0]
     features, capacity = returned_refs[0].shape
     total = jnp.zeros((features, rows), jnp.float32)
-    for bit in range(owners):
+    for k, bit in enumerate(return_order(owners)):
         spot = place_ref[0:1, :] - (me_ref[0] ^ bit) * capacity
         selector = hot(iota((capacity, rows), 0) == spot)
-        total += jnp.dot(returned_refs[bit][...], selector, preferred_element_type=jnp.float32)
+        total += jnp.dot(returned_refs[k][...], selector, preferred_element_type=jnp.float32)
     copy.wait()
     out_ref[...] = (held_ref[...] + ADAPTER_SCALE * total.T).astype(jnp.bfloat16)
 
@@ -540,7 +543,8 @@
         keep, give = late_down(bounds, side, adapter_row, held, early, (over, *late), rank, owners)
         mine, other = tensor_sum(keep, give)
         delta = up(me, side, adapter_row, up_rows, mine, other, owners)
-        returned = [delta[0]] + [exchange(delta[bit], "replica", bit) for bit in range(1, owners)]
+        returned = [exchange(delta[bit], "replica", bit) for bit in return_order(owners)[:-1]]
+        returned.append(delta[0])
         return unpack(me, place, returned, base)
 
     def to_one(owner):
@@ -585,6 +589,6 @@
         P("parts"),
     )
     out_specs = P(("parts", "replica"), "tensor")
-    small = mesh.shape["replica"] <= MAX_OWNERS and mesh.shape["tensor"] == 4
+    small = mesh.shape["replica"] in (2, 4, 8) and mesh.shape["tensor"] == 4
     chosen = body if small else plain_body
     return jax.shard_map(chosen, mesh=mesh, in_specs=in_specs, out_specs=out_specs, check_vma=False)

time: 107 us -> 107 us (level)
  starting transfers between devices: 37.2 us -> 38.8 us
    ppermute x8, starting transfers between devices: 23.3 us -> 24.6 us  [exchange(): return lax.ppermute(array, axis, [(k, k ^ bit) for k in range(size)])]
  transfers between devices with their start and end apart: 12 -> 12, of which waited for: 7 -> 7; matrix products, arithmetic and copies ran while one was open for 0% -> 0% of each run, Pallas kernels for 12% -> 11%
where the time goes in v1:
time: 107 us; the launch traced here: 106 us
  waiting for transfers between devices  44.7 us (42%)
  starting transfers between devices  38.8 us (36%)
  Pallas kernels  20.7 us (19%)
    all_to_all x1, waiting for transfers between devices, swap(): lax.all_to_all(array, 'replica', split_axis=0, concat_axis=0, tiled=True)  28 us
    ppermute x8, starting transfers between devices, exchange(): return lax.ppermute(array, axis, [(k, k ^ bit) for k in range(size)])  24.6 us
    ppermute x8, waiting for transfers between devices, exchange(): return lax.ppermute(array, axis, [(k, k ^ bit) for k in range(size)])  16.7 us
    ppermute x3, starting transfers between devices, send(): lax.ppermute(over, 'replica', [((owner - shift) % owners, owner)])  7.92 us
    pallas_call x1, Pallas kernels, early_down(): pl.pallas_call(functools.partial(early_kernel, rank, owners), in_specs=[p...  6.89 us
    all_to_all x1, starting transfers between devices, swap(): lax.all_to_all(array, 'replica', split_axis=0, concat_axis=0, tiled=True)  6.32 us
    pallas_call x1, Pallas kernels, route(): pl.pallas_call(functools.partial(route_kernel, owners, local_adapters), i...  4.95 us
    pallas_call x1, Pallas kernels, base_sum(): pl.pallas_call(base_kernel, in_specs=[smem, vmem, vmem], out_specs=[vmem]...  3.6 us
  transfers between devices with their start and end apart: 12, of which 7 were waited for; matrix products, arithmetic and copies ran while one was open for 0% of the time, Pallas kernels for 11%

profile of v1, /device:TPU:0, one launch (start us, length us, event | category | flops | bytes accessed | tf_op | source)
XLA Modules:
  0.0 105.8 jit_solution(4203662643946079304)
XLA Ops:
  0.0 0.0 copy-start.8
  0.0 0.0 copy-start.7
  0.0 4.9 %route.1 = (bf16[512,2048]{1,0:T(8,128)(2,1)}, bf16[128,2048]{1,0:T(8,128)(2,1)}, s32[8,512]{1,0:T(8,128)S(1)}, s32[1]{0:T(128)}) custom-call(s32[1]{0:T(128)} %bitcast.30.me_ref, s32[1,2048]{1,0:T(1,128)} %bitcast.104, s32[1,128]{1,0:T(1,128)} %bitcast.110, bf16[512,2048]{1,0:T(8,128)(2,1)} %tokens_ref.1), custom_call_target="tpu_custom_call" | custom-call | tf_op jit(solution)/shard_map/route/pallas_call | solution.py:177
  5.6 0.0 copy-done.8
  5.6 0.0 copy-done.7
  5.6 100.0 %conditional.1 = (bf16[512,128]{1,0:T(8,128)(2,1)}) conditional(s32[]{:T(128)} %bitcast.33, (s32[1]{0:T(128)}, s32[1,2048]{1,0:T(1,128)S(1)}, s32[1,128]{1,0:T(1,128)S(1)}, bf16[512,2048]{1,0:T(8,128)(2,1)}, bf16[2048,512]{1,0:T(8,128)(2,1)}, /*index=5*/bf16[512,2048]{1,0:T(8,128)(2,1)}, ...), branch_computations={%region_0.1_spmd, %region_1.2_spmd, %region_2.3_spmd, %region_3.4_... | conditional | flops 1075359744 | bytes 96934912 | solution.py:575
  5.8 6.3 %all-to-all-start.3 = ((bf16[4,128,2048]{2,1,0:T(8,128)(2,1)}), bf16[4,128,2048]{2,1,0:T(8,128)(2,1)S(1)}, u32[]{:S(2)}, u32[]{:S(2)}) async-start(bf16[4,128,2048]{2,1,0:T(8,128)(2,1)} %bitcast.96), calls=%async_computation.3 | async-start | bytes 4194304 | tf_op jit(solution)/shard_map/cond/branch_3_fun/all_to_all | solution.py:520
  12.2 3.6 %base.8 = (f32[512,128]{1,0:T(8,128)S(1)}, f32[512,128]{1,0:T(8,128)S(1)}, f32[2,512,128]{2,1,0:T(8,128)S(1)}) custom-call(s32[1]{0:T(128)} %bitcast.15.me_ref, bf16[512,2048]{1,0:T(8,128)(2,1)} %get-tuple-element.205.tokens_ref, bf16[2048,512]{1,0:T(8,128)(2,1)} %get-tuple-element.206.weight_ref), custom_call_target="tpu_custom_call" | custom-call | tf_op jit(solution)/shard_map/cond/branch_3_fun/base/pallas_call | solution.py:268
  15.8 0.1 collective-permute-start.33
  15.9 5.8 %collective-permute-start.37 = (bf16[128,2048]{1,0:T(8,128)(2,1)}, bf16[128,2048]{1,0:T(8,128)(2,1)S(1)}, u32[]{:S(2)}, u32[]{:S(2)}) collective-permute-start(bf16[128,2048]{1,0:T(8,128)(2,1)} %get-tuple-element.217.refs_5_), channel_id=1, source_target_pairs={{0,12},{1,13},{2,14},{3,15},{16,28},{17,29},{18,30},{19,31}} | collective-permute-start | bytes 1572872 | tf_op jit(solution)/shard_map/cond/branch_3_fun/ppermute | solution.py:553
  21.6 0.7 collective-permute-start.36
  22.3 1.5 %collective-permute-start.35 = (bf16[128,2048]{1,0:T(8,128)(2,1)}, bf16[128,2048]{1,0:T(8,128)(2,1)}, u32[]{:S(2)}, u32[]{:S(2)}) collective-permute-start(bf16[128,2048]{1,0:T(8,128)(2,1)} %get-tuple-element.217.refs_5_), channel_id=1, source_target_pairs={{8,12},{9,13},{10,14},{11,15},{24,28},{25,29},{26,30},{27,31}} | collective-permute-start | bytes 1572872 | tf_op jit(solution)/shard_map/cond/branch_3_fun/ppermute | solution.py:553
  23.8 0.0 collective-permute-done.33
  23.8 1.6 %collective-permute-start.34 = (f32[512,128]{1,0:T(8,128)S(1)}, f32[512,128]{1,0:T(8,128)S(1)}, u32[]{:S(2)}, u32[]{:S(2)}) collective-permute-start(f32[512,128]{1,0:T(8,128)S(1)} %fusion.9), channel_id=1, source_target_pairs={{0,2},{1,3},{2,0},{3,1},{4,6},{5,7},{6,4},{7,5},{8,10},{9,11},{10,... | collective-permute-start | bytes 786440 | tf_op jit(solution)/shard_map/cond/branch_3_fun/ppermute | solution.py:516
  25.4 1.3 %plan.8 = (s32[8,1024]{1,0:T(8,128)S(1)}, s32[8]{0:T(128)S(1)}) custom-call(s32[1]{0:T(128)} %get-tuple-element.199.me_ref, s32[1,2048]{1,0:T(1,128)S(1)} %get-tuple-element.202.request_ref, s32[1,128]{1,0:T(1,128)S(1)} %get-tuple-element.203.map_ref), custom_call_target="tpu_custom_call" | custom-call | tf_op jit(solution)/shard_map/cond/branch_3_fun/plan/pallas_call | solution.py:241
  26.7 5.6 %collective-permute-done.34 = f32[512,128]{1,0:T(8,128)S(1)} collective-permute-done((f32[512,128]{1,0:T(8,128)S(1)}, f32[512,128]{1,0:T(8,128)S(1)}, u32[]{:S(2)}, u32[]{:S(2)}) %collective-permute-start.34) | collective-permute-done | bytes 262176 | tf_op jit(solution)/shard_map/cond/branch_3_fun/ppermute | solution.py:516
  32.3 28.0 %all-to-all-done.3 = bf16[4,128,2048]{2,1,0:T(8,128)(2,1)S(1)} async-done(((bf16[4,128,2048]{2,1,0:T(8,128)(2,1)}), bf16[4,128,2048]{2,1,0:T(8,128)(2,1)S(1)}, u32[]{:S(2)}, u32[]{:S(2)}) %all-to-all-start.3) | async-done | bytes 2097184 | tf_op jit(solution)/shard_map/cond/branch_3_fun/all_to_all | solution.py:520
  60.4 6.9 %early_down.8 = (f32[64,512]{1,0:T(8,128)S(1)}, bf16[2048,2048]{1,0:T(8,128)(2,1)S(1)}) custom-call(s32[8]{0:T(128)S(1)} %get-tuple-element.212.bound_ref.refs_0_, s32[8,1024]{1,0:T(8,128)S(1)} %get-tuple-element.210.adapter_ref.refs_2_, bf16[2048,2048]{1,0:T(8,128)(2,1)} %get-tuple-element.213.down_ref, bf16[512,2048]{1,0:T(8,128)(2,1)S(1)} %bitcast.87), custom_call_target="tpu_custom_call" | custom-call | tf_op jit(solution)/shard_map/cond/branch_3_fun/early_down/pallas_call | solution.py:354
  67.3 0.0 collective-permute-done.37.refs_8_
  67.3 0.0 collective-permute-done.36.refs_7_
  67.3 0.0 collective-permute-done.35.refs_6_
  67.3 0.0 copy-start.5
  67.3 1.8 %late_down.8 = (f32[64,512]{1,0:T(8,128)S(1)}, f32[64,512]{1,0:T(8,128)S(1)}) custom-call(s32[8]{0:T(128)S(1)} %get-tuple-element.212.bound_ref.refs_0_, s32[1]{0:T(128)} %get-tuple-element.201.refs_1_.side_ref, s32[8,1024]{1,0:T(8,128)S(1)} %get-tuple-element.210.adapter_ref.refs_2_, bf16[2048,2048]{1,0:T(8,128)(2,1)S(1)} %get-tuple-element.215.refs_3_, ...), custom_call_target="tpu_custom_call" | custom-call | tf_op jit(solution)/shard_map/cond/branch_3_fun/late_down/pallas_call | solution.py:417
  69.2 0.1 collective-permute-start.38
  69.2 1.3 %collective-permute-done.38 = f32[64,512]{1,0:T(8,128)S(1)} collective-permute-done((f32[64,512]{1,0:T(8,128)S(1)}, f32[64,512]{1,0:T(8,128)S(1)}, u32[]{:S(2)}, u32[]{:S(2)}) %collective-permute-start.38) | collective-permute-done | bytes 131104 | tf_op jit(solution)/shard_map/cond/branch_3_fun/ppermute | solution.py:516
  70.6 1.6 %collective-permute-start.39 = (f32[64,512]{1,0:T(8,128)S(1)}, f32[64,512]{1,0:T(8,128)S(1)}, u32[]{:S(2)}, u32[]{:S(2)}) collective-permute-start(f32[64,512]{1,0:T(8,128)S(1)} %add.100), channel_id=1, source_target_pairs={{0,2},{1,3},{2,0},{3,1},{4,6},{5,7},{6,4},{7,5},{8,10},{9,11},{10,... | collective-permute-start | bytes 393224 | tf_op jit(solution)/shard_map/cond/branch_3_fun/ppermute | solution.py:516
  72.1 4.1 %collective-permute-done.39 = f32[64,512]{1,0:T(8,128)S(1)} collective-permute-done((f32[64,512]{1,0:T(8,128)S(1)}, f32[64,512]{1,0:T(8,128)S(1)}, u32[]{:S(2)}, u32[]{:S(2)}) %collective-permute-start.39) | collective-permute-done | bytes 131104 | tf_op jit(solution)/shard_map/cond/branch_3_fun/ppermute | solution.py:516
  76.2 0.1 collective-permute-start.40
  76.3 1.2 %collective-permute-done.40.other_ref = bf16[64,512]{1,0:T(8,128)(2,1)S(1)} collective-permute-done((bf16[64,512]{1,0:T(8,128)(2,1)S(1)}, bf16[64,512]{1,0:T(8,128)(2,1)S(1)}, u32[]{:S(2)}, u32[]{:S(2)}) %collective-permute-start.40) | collective-permute-done | bytes 65568 | tf_op jit(solution)/shard_map/cond/branch_3_fun/ppermute | solution.py:516
  77.5 0.0 copy-done.5
  77.5 0.9 up.8
  78.5 3.1 %collective-permute-start.41 = (bf16[128,256]{1,0:T(8,128)(2,1)S(1)}, bf16[128,256]{1,0:T(8,128)(2,1)S(1)}, u32[]{:S(2)}, u32[]{:S(2)}) collective-permute-start(bf16[128,256]{1,0:T(8,128)(2,1)S(1)} %get-tuple-element.220), channel_id=1, source_target_pairs={{0,8},{4,12},{8,0},{12,4},{1,9},{5,13},{9,1},{13,5},{2,10},{6,14},... | collective-permute-start | bytes 196616 | tf_op jit(solution)/shard_map/cond/branch_3_fun/ppermute | solution.py:516
  81.5 17.7 %collective-permute-start.42 = (bf16[128,256]{1,0:T(8,128)(2,1)S(1)}, bf16[128,256]{1,0:T(8,128)(2,1)S(1)}, u32[]{:S(2)}, u32[]{:S(2)}) collective-permute-start(bf16[128,256]{1,0:T(8,128)(2,1)S(1)} %get-tuple-element.221), channel_id=1, source_target_pairs={{0,12},{4,8},{8,4},{12,0},{1,13},{5,9},{9,5},{13,1},{2,14},{6,10},... | collective-permute-start | bytes 196616 | tf_op jit(solution)/shard_map/cond/branch_3_fun/ppermute | solution.py:516
  99.3 0.5 collective-permute-start.43
  99.8 0.0 collective-permute-done.41.refs_0_
  99.8 3.4 %collective-permute-done.42.refs_1_ = bf16[128,256]{1,0:T(8,128)(2,1)S(1)} collective-permute-done((bf16[128,256]{1,0:T(8,128)(2,1)S(1)}, bf16[128,256]{1,0:T(8,128)(2,1)S(1)}, u32[]{:S(2)}, u32[]{:S(2)}) %collective-permute-start.42) | collective-permute-done | bytes 65568 | tf_op jit(solution)/shard_map/cond/branch_3_fun/ppermute | solution.py:516
  103.2 1.1 %collective-permute-done.43.refs_2_ = bf16[128,256]{1,0:T(8,128)(2,1)S(1)} collective-permute-done((bf16[128,256]{1,0:T(8,128)(2,1)S(1)}, bf16[128,256]{1,0:T(8,128)(2,1)S(1)}, u32[]{:S(2)}, u32[]{:S(2)}) %collective-permute-start.43) | collective-permute-done | bytes 65568 | tf_op jit(solution)/shard_map/cond/branch_3_fun/ppermute | solution.py:516
  104.2 1.1 %unpack.8 = bf16[512,128]{1,0:T(8,128)(2,1)} custom-call(s32[1]{0:T(128)} %get-tuple-element.199.me_ref, s32[8,512]{1,0:T(8,128)S(1)} %get-tuple-element.200.place_ref, bf16[128,256]{1,0:T(8,128)(2,1)S(1)} %collective-permute-done.41.refs_0_, bf16[128,256]{1,0:T(8,128)(2,1)S(1)} %collective-permute-done.42.refs_1_, ...), custom_call_target="tpu_custom_call" | custom-call | tf_op jit(solution)/shard_map/cond/branch_3_fun/unpack/pallas_call | solution.py:502
  (4 shorter events, 0.1 us)
Async XLA Ops:
  0.0 5.6 %copy-start.8 = (s32[128]{0:T(128)S(1)}, s32[128]{0:T(128)}, u32[]{:S(2)}) copy-start(s32[128]{0:T(128)} %param.16) | copy-start | bytes 1540
  0.0 5.6 %copy-start.7 = (s32[2048]{0:T(1024)S(1)}, s32[2048]{0:T(1024)}, u32[]{:S(2)}) copy-start(s32[2048]{0:T(1024)} %param.15) | copy-start | bytes 24580
  5.8 54.5 %all-to-all-start.3 = ((bf16[4,128,2048]{2,1,0:T(8,128)(2,1)}), bf16[4,128,2048]{2,1,0:T(8,128)(2,1)S(1)}, u32[]{:S(2)}, u32[]{:S(2)}) async-start(bf16[4,128,2048]{2,1,0:T(8,128)(2,1)} %bitcast.96), calls=%async_computation.3 | async-start | bytes 4194304 | tf_op jit(solution)/shard_map/cond/branch_3_fun/all_to_all | solution.py:520
  15.8 8.0 %collective-permute-start.33 = (f32[2,512,128]{2,1,0:T(8,128)S(1)}, f32[2,512,128]{2,1,0:T(8,128)S(1)}, u32[]{:S(2)}, u32[]{:S(2)}) collective-permute-start(f32[2,512,128]{2,1,0:T(8,128)S(1)} %get-tuple-element.208), channel_id=1, source_target_pairs={{0,1},{1,0},{2,3},{3,2},{4,5},{5,4},{6,7},{7,6},{8,9},{9,8},{10,11... | collective-permute-start | bytes 1572872 | tf_op jit(solution)/shard_map/cond/branch_3_fun/ppermute | solution.py:516
  15.9 51.4 %collective-permute-start.37 = (bf16[128,2048]{1,0:T(8,128)(2,1)}, bf16[128,2048]{1,0:T(8,128)(2,1)S(1)}, u32[]{:S(2)}, u32[]{:S(2)}) collective-permute-start(bf16[128,2048]{1,0:T(8,128)(2,1)} %get-tuple-element.217.refs_5_), channel_id=1, source_target_pairs={{0,12},{1,13},{2,14},{3,15},{16,28},{17,29},{18,30},{19,31}} | collective-permute-start | bytes 1572872 | tf_op jit(solution)/shard_map/cond/branch_3_fun/ppermute | solution.py:553
  21.6 45.7 %collective-permute-start.36 = (bf16[128,2048]{1,0:T(8,128)(2,1)}, bf16[128,2048]{1,0:T(8,128)(2,1)S(1)}, u32[]{:S(2)}, u32[]{:S(2)}) collective-permute-start(bf16[128,2048]{1,0:T(8,128)(2,1)} %get-tuple-element.217.refs_5_), channel_id=1, source_target_pairs={{4,12},{5,13},{6,14},{7,15},{20,28},{21,29},{22,30},{23,31}} | collective-permute-start | bytes 1572872 | tf_op jit(solution)/shard_map/cond/branch_3_fun/ppermute | solution.py:553
  22.3 45.0 %collective-permute-start.35 = (bf16[128,2048]{1,0:T(8,128)(2,1)}, bf16[128,2048]{1,0:T(8,128)(2,1)}, u32[]{:S(2)}, u32[]{:S(2)}) collective-permute-start(bf16[128,2048]{1,0:T(8,128)(2,1)} %get-tuple-element.217.refs_5_), channel_id=1, source_target_pairs={{8,12},{9,13},{10,14},{11,15},{24,28},{25,29},{26,30},{27,31}} | collective-permute-start | bytes 1572872 | tf_op jit(solution)/shard_map/cond/branch_3_fun/ppermute | solution.py:553
  23.8 8.5 %collective-permute-start.34 = (f32[512,128]{1,0:T(8,128)S(1)}, f32[512,128]{1,0:T(8,128)S(1)}, u32[]{:S(2)}, u32[]{:S(2)}) collective-permute-start(f32[512,128]{1,0:T(8,128)S(1)} %fusion.9), channel_id=1, source_target_pairs={{0,2},{1,3},{2,0},{3,1},{4,6},{5,7},{6,4},{7,5},{8,10},{9,11},{10,... | collective-permute-start | bytes 786440 | tf_op jit(solution)/shard_map/cond/branch_3_fun/ppermute | solution.py:516
  67.3 10.3 %copy-start.5 = (bf16[2048,128]{1,0:T(8,128)(2,1)S(1)}, bf16[2048,128]{1,0:T(8,128)(2,1)}, u32[]{:S(2)}) copy-start(bf16[2048,128]{1,0:T(8,128)(2,1)} %get-tuple-element.211.up_ref) | copy-start | bytes 1572868 | tf_op jit(solution)/shard_map/cond
  69.2 1.4 %collective-permute-start.38 = (f32[64,512]{1,0:T(8,128)S(1)}, f32[64,512]{1,0:T(8,128)S(1)}, u32[]{:S(2)}, u32[]{:S(2)}) collective-permute-start(f32[64,512]{1,0:T(8,128)S(1)} %get-tuple-element.219), channel_id=1, source_target_pairs={{0,1},{1,0},{2,3},{3,2},{4,5},{5,4},{6,7},{7,6},{8,9},{9,8},{10,11... | collective-permute-start | bytes 393224 | tf_op jit(solution)/shard_map/cond/branch_3_fun/ppermute | solution.py:516
  70.6 5.6 %collective-permute-start.39 = (f32[64,512]{1,0:T(8,128)S(1)}, f32[64,512]{1,0:T(8,128)S(1)}, u32[]{:S(2)}, u32[]{:S(2)}) collective-permute-start(f32[64,512]{1,0:T(8,128)S(1)} %add.100), channel_id=1, source_target_pairs={{0,2},{1,3},{2,0},{3,1},{4,6},{5,7},{6,4},{7,5},{8,10},{9,11},{10,... | collective-permute-start | bytes 393224 | tf_op jit(solution)/shard_map/cond/branch_3_fun/ppermute | solution.py:516
  76.2 1.3 %collective-permute-start.40 = (bf16[64,512]{1,0:T(8,128)(2,1)S(1)}, bf16[64,512]{1,0:T(8,128)(2,1)S(1)}, u32[]{:S(2)}, u32[]{:S(2)}) collective-permute-start(bf16[64,512]{1,0:T(8,128)(2,1)S(1)} %add_convert_fusion.3.mine_ref), channel_id=1, source_target_pairs={{0,1},{1,0},{2,3},{3,2},{4,5},{5,4},{6,7},{7,6},{8,9},{9,8},{10,11... | collective-permute-start | bytes 196616 | tf_op jit(solution)/shard_map/cond/branch_3_fun/ppermute | solution.py:516
  78.5 21.3 %collective-permute-start.41 = (bf16[128,256]{1,0:T(8,128)(2,1)S(1)}, bf16[128,256]{1,0:T(8,128)(2,1)S(1)}, u32[]{:S(2)}, u32[]{:S(2)}) collective-permute-start(bf16[128,256]{1,0:T(8,128)(2,1)S(1)} %get-tuple-element.220), channel_id=1, source_target_pairs={{0,8},{4,12},{8,0},{12,4},{1,9},{5,13},{9,1},{13,5},{2,10},{6,14},... | collective-permute-start | bytes 196616 | tf_op jit(solution)/shard_map/cond/branch_3_fun/ppermute | solution.py:516
  81.5 21.6 %collective-permute-start.42 = (bf16[128,256]{1,0:T(8,128)(2,1)S(1)}, bf16[128,256]{1,0:T(8,128)(2,1)S(1)}, u32[]{:S(2)}, u32[]{:S(2)}) collective-permute-start(bf16[128,256]{1,0:T(8,128)(2,1)S(1)} %get-tuple-element.221), channel_id=1, source_target_pairs={{0,12},{4,8},{8,4},{12,0},{1,13},{5,9},{9,5},{13,1},{2,14},{6,10},... | collective-permute-start | bytes 196616 | tf_op jit(solution)/shard_map/cond/branch_3_fun/ppermute | solution.py:516
  99.3 5.0 %collective-permute-start.43 = (bf16[128,256]{1,0:T(8,128)(2,1)S(1)}, bf16[128,256]{1,0:T(8,128)(2,1)S(1)}, u32[]{:S(2)}, u32[]{:S(2)}) collective-permute-start(bf16[128,256]{1,0:T(8,128)(2,1)S(1)} %get-tuple-element.222), channel_id=1, source_target_pairs={{0,4},{4,0},{8,12},{12,8},{1,5},{5,1},{9,13},{13,9},{2,6},{6,2},{1... | collective-permute-start | bytes 196616 | tf_op jit(solution)/shard_map/cond/branch_3_fun/ppermute | solution.py:516

commit v2 on v1

--- a/solution.py
+++ b/solution.py
@@ -145,7 +145,7 @@
     counts = jnp.sum(jnp.where(mine, 1.0, 0.0), axis=1, keepdims=True)
     row, column = iota((pool, pool), 0), iota((pool, pool), 1)
     same = lax.div(row, jnp.int32(local_adapters)) == lax.div(column, jnp.int32(local_adapters))
-    ranks += column_sums(hot(same & (column < row)), counts)
+    ranks += column_sums(hot(same & (column > row)), counts)
     rank = jnp.sum(jnp.where(mine, ranks, 0.0), axis=0, keepdims=True).astype(jnp.int32)
     owner = lax.div(slot, jnp.int32(local_adapters))
     place_ref[...] = jnp.broadcast_to(owner * capacity + rank, (8, rows))
@@ -204,16 +204,16 @@
     capacity = 2 * rows // owners
     slots, _ = lookup(request_ref, map_ref, owners, local_adapters)
     shape = (local_adapters, local_adapters)
-    upto = hot(iota(shape, 1) <= iota(shape, 0))
+    onward = hot(iota(shape, 1) >= iota(shape, 0))
     place = iota((local_adapters, capacity), 1)
     found = []
     for source in range(owners):
         slot = slots[:, source * rows : (source + 1) * rows]
         mine = iota((local_adapters, rows), 0) + me * local_adapters == slot
         counts = jnp.sum(jnp.where(mine, 1.0, 0.0), axis=1, keepdims=True)
-        ends = column_sums(upto, counts).astype(jnp.int32)
+        ends = column_sums(onward, counts).astype(jnp.int32)
         passed = jnp.sum(jnp.where(ends <= place, 1, 0), axis=0, keepdims=True)
-        found.append(jnp.where(passed < local_adapters, passed, -1))
+        found.append(local_adapters - 1 - passed)
     size = capacity // GROUPS
     for group in range(GROUPS):
         span = slice(group * size, (group + 1) * size)

time: 107 us -> 105 us (0.981)
  starting transfers between devices: 38.8 us -> 17.1 us
  waiting for transfers between devices: 44.7 us -> 64.4 us
    ppermute x8, starting transfers between devices: 24.6 us -> 6.87 us  [exchange(): return lax.ppermute(array, axis, [(k, k ^ bit) for k in range(size)])]
    all_to_all x1, waiting for transfers between devices: 28 us -> 44 us  [swap(): lax.all_to_all(array, 'replica', split_axis=0, concat_axis=0, tiled=True)]
    ppermute x3, starting transfers between devices: 7.92 us -> 3.88 us  [send(): lax.ppermute(over, 'replica', [((owner - shift) % owners, owner)])]
    ppermute x3, waiting for transfers between devices: 0.01 us -> 3.48 us  [send(): lax.ppermute(over, 'replica', [((owner - shift) % owners, owner)])]
    pallas_call x1, Pallas kernels: 1.84 us -> 3.09 us  [late_down(): pl.pallas_call(functools.partial(late_kernel, rank, owners), in_specs=[sm...]
  transfers between devices with their start and end apart: 12 -> 12, of which waited for: 7 -> 8; matrix products, arithmetic and copies ran while one was open for 0% -> 0% of each run, Pallas kernels for 11% -> 11%
where the time goes in v2:
time: 105 us
  waiting for transfers between devices  64.4 us (61%)
  Pallas kernels  21.7 us (21%)
  starting transfers between devices  17.1 us (16%)
    all_to_all x1, waiting for transfers between devices, swap(): lax.all_to_all(array, 'replica', split_axis=0, concat_axis=0, tiled=True)  44 us
    ppermute x8, waiting for transfers between devices, exchange(): return lax.ppermute(array, axis, [(k, k ^ bit) for k in range(size)])  16.9 us
    ppermute x8, starting transfers between devices, exchange(): return lax.ppermute(array, axis, [(k, k ^ bit) for k in range(size)])  6.87 us
    pallas_call x1, Pallas kernels, early_down(): pl.pallas_call(functools.partial(early_kernel, rank, owners), in_specs=[p...  6.7 us
    all_to_all x1, starting transfers between devices, swap(): lax.all_to_all(array, 'replica', split_axis=0, concat_axis=0, tiled=True)  6.32 us
    pallas_call x1, Pallas kernels, route(): pl.pallas_call(functools.partial(route_kernel, owners, local_adapters), i...  4.95 us
    ppermute x3, starting transfers between devices, send(): lax.ppermute(over, 'replica', [((owner - shift) % owners, owner)])  3.88 us
    pallas_call x1, Pallas kernels, base_sum(): pl.pallas_call(base_kernel, in_specs=[smem, vmem, vmem], out_specs=[vmem]...  3.6 us
  transfers between devices with their start and end apart: 12, of which 8 were waited for; matrix products, arithmetic and copies ran while one was open for 0% of the time, Pallas kernels for 11%

profile of v2, /device:TPU:0, one launch (start us, length us, event | category | flops | bytes accessed | tf_op | source)
XLA Modules:
  0.0 104.8 jit_solution(7719734873371846820)
XLA Ops:
  0.0 0.0 copy-start.8
  0.0 0.0 copy-start.7
  0.0 4.9 %route.1 = (bf16[512,2048]{1,0:T(8,128)(2,1)}, bf16[128,2048]{1,0:T(8,128)(2,1)}, s32[8,512]{1,0:T(8,128)S(1)}, s32[1]{0:T(128)}) custom-call(s32[1]{0:T(128)} %bitcast.30.me_ref, s32[1,2048]{1,0:T(1,128)} %bitcast.104, s32[1,128]{1,0:T(1,128)} %bitcast.110, bf16[512,2048]{1,0:T(8,128)(2,1)} %tokens_ref.1), custom_call_target="tpu_custom_call" | custom-call | tf_op jit(solution)/shard_map/route/pallas_call | solution.py:177
  5.6 0.0 copy-done.8
  5.6 0.0 copy-done.7
  5.6 99.0 %conditional.1 = (bf16[512,128]{1,0:T(8,128)(2,1)}) conditional(s32[]{:T(128)} %bitcast.33, (s32[1]{0:T(128)}, s32[1,2048]{1,0:T(1,128)S(1)}, s32[1,128]{1,0:T(1,128)S(1)}, bf16[512,2048]{1,0:T(8,128)(2,1)}, bf16[2048,512]{1,0:T(8,128)(2,1)}, /*index=5*/bf16[512,2048]{1,0:T(8,128)(2,1)}, ...), branch_computations={%region_0.1_spmd, %region_1.2_spmd, %region_2.3_spmd, %region_3.4_... | conditional | flops 1075359744 | bytes 96934912 | solution.py:575
  5.6 6.3 %all-to-all-start = ((bf16[4,128,2048]{2,1,0:T(8,128)(2,1)}), bf16[4,128,2048]{2,1,0:T(8,128)(2,1)S(1)}, u32[]{:S(2)}, u32[]{:S(2)}) async-start(bf16[4,128,2048]{2,1,0:T(8,128)(2,1)} %bitcast.93), calls=%async_computation | async-start | bytes 4194304 | tf_op jit(solution)/shard_map/cond/branch_0_fun/all_to_all | solution.py:520
  12.0 3.6 %base.5 = (f32[512,128]{1,0:T(8,128)S(1)}, f32[512,128]{1,0:T(8,128)S(1)}, f32[2,512,128]{2,1,0:T(8,128)S(1)}) custom-call(s32[1]{0:T(128)} %bitcast.me_ref, bf16[512,2048]{1,0:T(8,128)(2,1)} %get-tuple-element.127.tokens_ref, bf16[2048,512]{1,0:T(8,128)(2,1)} %get-tuple-element.128.weight_ref), custom_call_target="tpu_custom_call" | custom-call | tf_op jit(solution)/shard_map/cond/branch_0_fun/base/pallas_call | solution.py:268
  15.6 0.1 collective-permute-start
  15.7 1.3 %collective-permute-start.4 = (bf16[128,2048]{1,0:T(8,128)(2,1)}, bf16[128,2048]{1,0:T(8,128)(2,1)S(1)}, u32[]{:S(2)}, u32[]{:S(2)}) collective-permute-start(bf16[128,2048]{1,0:T(8,128)(2,1)} %get-tuple-element.139.refs_5_), channel_id=1, source_target_pairs={{4,0},{5,1},{6,2},{7,3},{20,16},{21,17},{22,18},{23,19}} | collective-permute-start | bytes 1572872 | tf_op jit(solution)/shard_map/cond/branch_0_fun/ppermute | solution.py:553
  17.0 1.3 %collective-permute-start.3 = (bf16[128,2048]{1,0:T(8,128)(2,1)}, bf16[128,2048]{1,0:T(8,128)(2,1)S(1)}, u32[]{:S(2)}, u32[]{:S(2)}) collective-permute-start(bf16[128,2048]{1,0:T(8,128)(2,1)} %get-tuple-element.139.refs_5_), channel_id=1, source_target_pairs={{8,0},{9,1},{10,2},{11,3},{24,16},{25,17},{26,18},{27,19}} | collective-permute-start | bytes 1572872 | tf_op jit(solution)/shard_map/cond/branch_0_fun/ppermute | solution.py:553
  18.3 1.3 %collective-permute-start.2 = (bf16[128,2048]{1,0:T(8,128)(2,1)}, bf16[128,2048]{1,0:T(8,128)(2,1)}, u32[]{:S(2)}, u32[]{:S(2)}) collective-permute-start(bf16[128,2048]{1,0:T(8,128)(2,1)} %get-tuple-element.139.refs_5_), channel_id=1, source_target_pairs={{12,0},{13,1},{14,2},{15,3},{28,16},{29,17},{30,18},{31,19}} | collective-permute-start | bytes 1572872 | tf_op jit(solution)/shard_map/cond/branch_0_fun/ppermute | solution.py:553
  19.6 0.0 collective-permute-done
  19.6 1.6 %collective-permute-start.1 = (f32[512,128]{1,0:T(8,128)S(1)}, f32[512,128]{1,0:T(8,128)S(1)}, u32[]{:S(2)}, u32[]{:S(2)}) collective-permute-start(f32[512,128]{1,0:T(8,128)S(1)} %fusion), channel_id=1, source_target_pairs={{0,2},{1,3},{2,0},{3,1},{4,6},{5,7},{6,4},{7,5},{8,10},{9,11},{10,... | collective-permute-start | bytes 786440 | tf_op jit(solution)/shard_map/cond/branch_0_fun/ppermute | solution.py:516
  21.2 1.3 %plan.5 = (s32[8,1024]{1,0:T(8,128)S(1)}, s32[8]{0:T(128)S(1)}) custom-call(s32[1]{0:T(128)} %get-tuple-element.98.me_ref, s32[1,2048]{1,0:T(1,128)S(1)} %get-tuple-element.124.request_ref, s32[1,128]{1,0:T(1,128)S(1)} %get-tuple-element.125.map_ref), custom_call_target="tpu_custom_call" | custom-call | tf_op jit(solution)/shard_map/cond/branch_0_fun/plan/pallas_call | solution.py:241
  22.5 5.9 %collective-permute-done.1 = f32[512,128]{1,0:T(8,128)S(1)} collective-permute-done((f32[512,128]{1,0:T(8,128)S(1)}, f32[512,128]{1,0:T(8,128)S(1)}, u32[]{:S(2)}, u32[]{:S(2)}) %collective-permute-start.1) | collective-permute-done | bytes 262176 | tf_op jit(solution)/shard_map/cond/branch_0_fun/ppermute | solution.py:516
  28.4 44.0 %all-to-all-done = bf16[4,128,2048]{2,1,0:T(8,128)(2,1)S(1)} async-done(((bf16[4,128,2048]{2,1,0:T(8,128)(2,1)}), bf16[4,128,2048]{2,1,0:T(8,128)(2,1)S(1)}, u32[]{:S(2)}, u32[]{:S(2)}) %all-to-all-start) | async-done | bytes 2097184 | tf_op jit(solution)/shard_map/cond/branch_0_fun/all_to_all | solution.py:520
  72.4 6.7 %early_down.5 = (f32[64,512]{1,0:T(8,128)S(1)}, bf16[2048,2048]{1,0:T(8,128)(2,1)S(1)}) custom-call(s32[8]{0:T(128)S(1)} %get-tuple-element.134.bound_ref.refs_0_, s32[8,1024]{1,0:T(8,128)S(1)} %get-tuple-element.132.adapter_ref.refs_2_, bf16[2048,2048]{1,0:T(8,128)(2,1)} %get-tuple-element.135.down_ref, bf16[512,2048]{1,0:T(8,128)(2,1)S(1)} %bitcast.84), custom_call_target="tpu_custom_call" | custom-call | tf_op jit(solution)/shard_map/cond/branch_0_fun/early_down/pallas_call | solution.py:354
  79.2 0.0 collective-permute-done.4.refs_8_
  79.2 3.5 %collective-permute-done.3.refs_7_ = bf16[128,2048]{1,0:T(8,128)(2,1)S(1)} collective-permute-done((bf16[128,2048]{1,0:T(8,128)(2,1)}, bf16[128,2048]{1,0:T(8,128)(2,1)S(1)}, u32[]{:S(2)}, u32[]{:S(2)}) %collective-permute-start.3) | collective-permute-done | bytes 524320 | tf_op jit(solution)/shard_map/cond/branch_0_fun/ppermute | solution.py:553
  82.6 0.0 collective-permute-done.2.refs_6_
  82.6 0.0 copy-start.2
  82.7 3.1 %late_down.5 = (f32[64,512]{1,0:T(8,128)S(1)}, f32[64,512]{1,0:T(8,128)S(1)}) custom-call(s32[8]{0:T(128)S(1)} %get-tuple-element.134.bound_ref.refs_0_, s32[1]{0:T(128)} %get-tuple-element.122.refs_1_.side_ref, s32[8,1024]{1,0:T(8,128)S(1)} %get-tuple-element.132.adapter_ref.refs_2_, bf16[2048,2048]{1,0:T(8,128)(2,1)S(1)} %get-tuple-element.137.refs_3_, ...), custom_call_target="tpu_custom_call" | custom-call | tf_op jit(solution)/shard_map/cond/branch_0_fun/late_down/pallas_call | solution.py:417
  85.8 0.1 collective-permute-start.5
  85.8 1.3 %collective-permute-done.5 = f32[64,512]{1,0:T(8,128)S(1)} collective-permute-done((f32[64,512]{1,0:T(8,128)S(1)}, f32[64,512]{1,0:T(8,128)S(1)}, u32[]{:S(2)}, u32[]{:S(2)}) %collective-permute-start.5) | collective-permute-done | bytes 131104 | tf_op jit(solution)/shard_map/cond/branch_0_fun/ppermute | solution.py:516
  87.2 1.6 %collective-permute-start.6 = (f32[64,512]{1,0:T(8,128)S(1)}, f32[64,512]{1,0:T(8,128)S(1)}, u32[]{:S(2)}, u32[]{:S(2)}) collective-permute-start(f32[64,512]{1,0:T(8,128)S(1)} %add.85), channel_id=1, source_target_pairs={{0,2},{1,3},{2,0},{3,1},{4,6},{5,7},{6,4},{7,5},{8,10},{9,11},{10,... | collective-permute-start | bytes 393224 | tf_op jit(solution)/shard_map/cond/branch_0_fun/ppermute | solution.py:516
  88.7 4.1 %collective-permute-done.6 = f32[64,512]{1,0:T(8,128)S(1)} collective-permute-done((f32[64,512]{1,0:T(8,128)S(1)}, f32[64,512]{1,0:T(8,128)S(1)}, u32[]{:S(2)}, u32[]{:S(2)}) %collective-permute-start.6) | collective-permute-done | bytes 131104 | tf_op jit(solution)/shard_map/cond/branch_0_fun/ppermute | solution.py:516
  92.8 0.1 collective-permute-start.7
  92.9 1.2 %collective-permute-done.7.other_ref = bf16[64,512]{1,0:T(8,128)(2,1)S(1)} collective-permute-done((bf16[64,512]{1,0:T(8,128)(2,1)S(1)}, bf16[64,512]{1,0:T(8,128)(2,1)S(1)}, u32[]{:S(2)}, u32[]{:S(2)}) %collective-permute-start.7) | collective-permute-done | bytes 65568 | tf_op jit(solution)/shard_map/cond/branch_0_fun/ppermute | solution.py:516
  94.1 0.0 copy-done.2
  94.1 0.9 up.5
  95.1 0.1 collective-permute-start.8
  95.1 0.1 collective-permute-start.9
  95.2 3.4 %collective-permute-start.10 = (bf16[128,256]{1,0:T(8,128)(2,1)S(1)}, bf16[128,256]{1,0:T(8,128)(2,1)S(1)}, u32[]{:S(2)}, u32[]{:S(2)}) collective-permute-start(bf16[128,256]{1,0:T(8,128)(2,1)S(1)} %get-tuple-element.144), channel_id=1, source_target_pairs={{0,4},{4,0},{8,12},{12,8},{1,5},{5,1},{9,13},{13,9},{2,6},{6,2},{1... | collective-permute-start | bytes 196616 | tf_op jit(solution)/shard_map/cond/branch_0_fun/ppermute | solution.py:516
  98.6 3.7 %collective-permute-done.8.refs_0_ = bf16[128,256]{1,0:T(8,128)(2,1)S(1)} collective-permute-done((bf16[128,256]{1,0:T(8,128)(2,1)S(1)}, bf16[128,256]{1,0:T(8,128)(2,1)S(1)}, u32[]{:S(2)}, u32[]{:S(2)}) %collective-permute-start.8) | collective-permute-done | bytes 65568 | tf_op jit(solution)/shard_map/cond/branch_0_fun/ppermute | solution.py:516
  102.3 0.0 collective-permute-done.9.refs_1_
  102.3 0.7 collective-permute-done.10.refs_2_
  103.0 1.1 %unpack.5 = bf16[512,128]{1,0:T(8,128)(2,1)} custom-call(s32[1]{0:T(128)} %get-tuple-element.98.me_ref, s32[8,512]{1,0:T(8,128)S(1)} %get-tuple-element.120.place_ref, bf16[128,256]{1,0:T(8,128)(2,1)S(1)} %collective-permute-done.8.refs_0_, bf16[128,256]{1,0:T(8,128)(2,1)S(1)} %collective-permute-done.9.refs_1_, ...), custom_call_target="tpu_custom_call" | custom-call | tf_op jit(solution)/shard_map/cond/branch_0_fun/unpack/pallas_call | solution.py:502
  (4 shorter events, 0.1 us)
Async XLA Ops:
  0.0 5.6 %copy-start.8 = (s32[128]{0:T(128)S(1)}, s32[128]{0:T(128)}, u32[]{:S(2)}) copy-start(s32[128]{0:T(128)} %param.16) | copy-start | bytes 1540
  0.0 5.6 %copy-start.7 = (s32[2048]{0:T(1024)S(1)}, s32[2048]{0:T(1024)}, u32[]{:S(2)}) copy-start(s32[2048]{0:T(1024)} %param.15) | copy-start | bytes 24580
  5.6 66.8 %all-to-all-start = ((bf16[4,128,2048]{2,1,0:T(8,128)(2,1)}), bf16[4,128,2048]{2,1,0:T(8,128)(2,1)S(1)}, u32[]{:S(2)}, u32[]{:S(2)}) async-start(bf16[4,128,2048]{2,1,0:T(8,128)(2,1)} %bitcast.93), calls=%async_computation | async-start | bytes 4194304 | tf_op jit(solution)/shard_map/cond/branch_0_fun/all_to_all | solution.py:520
  15.6 4.0 %collective-permute-start = (f32[2,512,128]{2,1,0:T(8,128)S(1)}, f32[2,512,128]{2,1,0:T(8,128)S(1)}, u32[]{:S(2)}, u32[]{:S(2)}) collective-permute-start(f32[2,512,128]{2,1,0:T(8,128)S(1)} %get-tuple-element.130), channel_id=1, source_target_pairs={{0,1},{1,0},{2,3},{3,2},{4,5},{5,4},{6,7},{7,6},{8,9},{9,8},{10,11... | collective-permute-start | bytes 1572872 | tf_op jit(solution)/shard_map/cond/branch_0_fun/ppermute | solution.py:516
  15.7 63.5 %collective-permute-start.4 = (bf16[128,2048]{1,0:T(8,128)(2,1)}, bf16[128,2048]{1,0:T(8,128)(2,1)S(1)}, u32[]{:S(2)}, u32[]{:S(2)}) collective-permute-start(bf16[128,2048]{1,0:T(8,128)(2,1)} %get-tuple-element.139.refs_5_), channel_id=1, source_target_pairs={{4,0},{5,1},{6,2},{7,3},{20,16},{21,17},{22,18},{23,19}} | collective-permute-start | bytes 1572872 | tf_op jit(solution)/shard_map/cond/branch_0_fun/ppermute | solution.py:553
  17.0 65.7 %collective-permute-start.3 = (bf16[128,2048]{1,0:T(8,128)(2,1)}, bf16[128,2048]{1,0:T(8,128)(2,1)S(1)}, u32[]{:S(2)}, u32[]{:S(2)}) collective-permute-start(bf16[128,2048]{1,0:T(8,128)(2,1)} %get-tuple-element.139.refs_5_), channel_id=1, source_target_pairs={{8,0},{9,1},{10,2},{11,3},{24,16},{25,17},{26,18},{27,19}} | collective-permute-start | bytes 1572872 | tf_op jit(solution)/shard_map/cond/branch_0_fun/ppermute | solution.py:553
  18.3 64.4 %collective-permute-start.2 = (bf16[128,2048]{1,0:T(8,128)(2,1)}, bf16[128,2048]{1,0:T(8,128)(2,1)}, u32[]{:S(2)}, u32[]{:S(2)}) collective-permute-start(bf16[128,2048]{1,0:T(8,128)(2,1)} %get-tuple-element.139.refs_5_), channel_id=1, source_target_pairs={{12,0},{13,1},{14,2},{15,3},{28,16},{29,17},{30,18},{31,19}} | collective-permute-start | bytes 1572872 | tf_op jit(solution)/shard_map/cond/branch_0_fun/ppermute | solution.py:553
  19.6 8.8 %collective-permute-start.1 = (f32[512,128]{1,0:T(8,128)S(1)}, f32[512,128]{1,0:T(8,128)S(1)}, u32[]{:S(2)}, u32[]{:S(2)}) collective-permute-start(f32[512,128]{1,0:T(8,128)S(1)} %fusion), channel_id=1, source_target_pairs={{0,2},{1,3},{2,0},{3,1},{4,6},{5,7},{6,4},{7,5},{8,10},{9,11},{10,... | collective-permute-start | bytes 786440 | tf_op jit(solution)/shard_map/cond/branch_0_fun/ppermute | solution.py:516
  82.6 11.5 %copy-start.2 = (bf16[2048,128]{1,0:T(8,128)(2,1)S(1)}, bf16[2048,128]{1,0:T(8,128)(2,1)}, u32[]{:S(2)}) copy-start(bf16[2048,128]{1,0:T(8,128)(2,1)} %get-tuple-element.133.up_ref) | copy-start | bytes 1572868 | tf_op jit(solution)/shard_map/cond
  85.8 1.4 %collective-permute-start.5 = (f32[64,512]{1,0:T(8,128)S(1)}, f32[64,512]{1,0:T(8,128)S(1)}, u32[]{:S(2)}, u32[]{:S(2)}) collective-permute-start(f32[64,512]{1,0:T(8,128)S(1)} %get-tuple-element.141), channel_id=1, source_target_pairs={{0,1},{1,0},{2,3},{3,2},{4,5},{5,4},{6,7},{7,6},{8,9},{9,8},{10,11... | collective-permute-start | bytes 393224 | tf_op jit(solution)/shard_map/cond/branch_0_fun/ppermute | solution.py:516
  87.2 5.6 %collective-permute-start.6 = (f32[64,512]{1,0:T(8,128)S(1)}, f32[64,512]{1,0:T(8,128)S(1)}, u32[]{:S(2)}, u32[]{:S(2)}) collective-permute-start(f32[64,512]{1,0:T(8,128)S(1)} %add.85), channel_id=1, source_target_pairs={{0,2},{1,3},{2,0},{3,1},{4,6},{5,7},{6,4},{7,5},{8,10},{9,11},{10,... | collective-permute-start | bytes 393224 | tf_op jit(solution)/shard_map/cond/branch_0_fun/ppermute | solution.py:516
  92.8 1.3 %collective-permute-start.7 = (bf16[64,512]{1,0:T(8,128)(2,1)S(1)}, bf16[64,512]{1,0:T(8,128)(2,1)S(1)}, u32[]{:S(2)}, u32[]{:S(2)}) collective-permute-start(bf16[64,512]{1,0:T(8,128)(2,1)S(1)} %add_convert_fusion.mine_ref), channel_id=1, source_target_pairs={{0,1},{1,0},{2,3},{3,2},{4,5},{5,4},{6,7},{7,6},{8,9},{9,8},{10,11... | collective-permute-start | bytes 196616 | tf_op jit(solution)/shard_map/cond/branch_0_fun/ppermute | solution.py:516
  95.1 7.2 %collective-permute-start.8 = (bf16[128,256]{1,0:T(8,128)(2,1)S(1)}, bf16[128,256]{1,0:T(8,128)(2,1)S(1)}, u32[]{:S(2)}, u32[]{:S(2)}) collective-permute-start(bf16[128,256]{1,0:T(8,128)(2,1)S(1)} %get-tuple-element.142), channel_id=1, source_target_pairs={{0,8},{4,12},{8,0},{12,4},{1,9},{5,13},{9,1},{13,5},{2,10},{6,14},... | collective-permute-start | bytes 196616 | tf_op jit(solution)/shard_map/cond/branch_0_fun/ppermute | solution.py:516
  95.1 7.2 %collective-permute-start.9 = (bf16[128,256]{1,0:T(8,128)(2,1)S(1)}, bf16[128,256]{1,0:T(8,128)(2,1)S(1)}, u32[]{:S(2)}, u32[]{:S(2)}) collective-permute-start(bf16[128,256]{1,0:T(8,128)(2,1)S(1)} %get-tuple-element.143), channel_id=1, source_target_pairs={{0,12},{4,8},{8,4},{12,0},{1,13},{5,9},{9,5},{13,1},{2,14},{6,10},... | collective-permute-start | bytes 196616 | tf_op jit(solution)/shard_map/cond/branch_0_fun/ppermute | solution.py:516
  95.2 7.8 %collective-permute-start.10 = (bf16[128,256]{1,0:T(8,128)(2,1)S(1)}, bf16[128,256]{1,0:T(8,128)(2,1)S(1)}, u32[]{:S(2)}, u32[]{:S(2)}) collective-permute-start(bf16[128,256]{1,0:T(8,128)(2,1)S(1)} %get-tuple-element.144), channel_id=1, source_target_pairs={{0,4},{4,0},{8,12},{12,8},{1,5},{5,1},{9,13},{13,9},{2,6},{6,2},{1... | collective-permute-start | bytes 196616 | tf_op jit(solution)/shard_map/cond/branch_0_fun/ppermute | solution.py:516
